TPU v7x, 32 devices: a whole 2x2x4 slice. The times are simulated.
32 devices in a mesh: row: 4 (over y, x), col: 8 (over z, core).
Axes of the slice: x: 2, y: 2, z: 4, core: 2. Of those that a mesh axis runs over, the one named last changes fastest.
Arguments:
- inputs: bfloat16 [128, 448, 128], P('row', 'col'), may hold values from -6 to 6
- cotangent: bfloat16 [128, 448, 128], P('row', 'col'), may hold values from -6 to 6
- w_conv: bfloat16 [3, 3, 128, 128], replicated, may hold values from -0.1875 to 0.1875
- w_down: bfloat16 [3, 3, 128, 256], replicated, may hold values from -0.1875 to 0.1875
- w_up: bfloat16 [2, 2, 256, 128], replicated, may hold values from -0.375 to 0.375
Outputs:
- output: bfloat16 [128, 448, 128], P('row', 'col')
- grad_inputs: bfloat16 [128, 448, 128], P('row', 'col')
- grad_conv: float32 [147456], P(('row', 'col'))
- grad_down: float32 [294912], P(('row', 'col'))
- grad_up: float32 [131072], P(('row', 'col'))
All inputs are finite; a program needn't handle non-finite values.
Results may differ from a plain program's by a relative error of at most 0.013.
Values may be sent and summed in bfloat16 or wider, within the bound.
A program may use at most 64 MiB of HBM per device.

v0:
```python
import math

import jax
import jax.numpy as jnp
from jax import lax
from jax.sharding import PartitionSpec as P


def extended(block, sides, width):
    for axis, dim in sides:
        count = lax.axis_size(axis)
        forward = [(i, i + 1) for i in range(count - 1)]
        backward = [(target, source) for source, target in forward]
        low = lax.ppermute(
            lax.slice_in_dim(block, block.shape[dim] - width, None, axis=dim), axis, forward
        )
        high = lax.ppermute(lax.slice_in_dim(block, 0, width, axis=dim), axis, backward)
        block = jnp.concatenate([low, block, high], axis=dim)
    return block


def from_behind(value, axis, steps):
    count = lax.axis_size(axis)
    leading, last = (max(0, -steps), min(count, count - steps))
    return lax.ppermute(value, axis, [(source, source + steps) for source in range(leading, last)])


def silu_slope(value):
    sig = jax.nn.sigmoid(value)
    return sig * (1.0 + value * (1.0 - sig))


def conv_taps(padded, kernel, count_r, count_c):
    width = padded.shape[2]
    total = None
    for pos_r in range(3):
        for pos_c in range(3):
            window = padded[pos_r : pos_r + count_r, pos_c : pos_c + count_c].reshape(-1, width)
            term = jnp.dot(window, kernel[pos_r, pos_c], preferred_element_type=jnp.float32)
            total = term if total is None else total + term
    return total.reshape(count_r, count_c, -1)


def body(inputs, cotangent, w_conv, w_down, w_up):
    rows, cols, width = inputs.shape
    wide = w_down.shape[3]
    half_r = rows // 2
    half_c = cols // 2
    n_row = lax.axis_size("row")
    n_col = lax.axis_size("col")
    padded = extended(inputs, (("row", 0), ("col", 1)), 1)
    pre = conv_taps(padded, w_conv, rows, cols)
    fine_own = jax.nn.silu(pre).astype(jnp.bfloat16)
    top = from_behind(fine_own[-1:], "row", 1)
    fine_rows = jnp.concatenate([top, fine_own], axis=0)
    left = from_behind(fine_rows[:, -1:], "col", 1)
    fine_ext = jnp.concatenate([left, fine_rows], axis=1)
    fine = fine_ext[1:, 1:]
    strided = {}
    coarse_pre = None
    for pos_r in range(3):
        for pos_c in range(3):
            window = fine_ext[
                pos_r : pos_r + 2 * half_r - 1 : 2, pos_c : pos_c + 2 * half_c - 1 : 2
            ].reshape(-1, width)
            strided[pos_r, pos_c] = window
            term = jnp.dot(window, w_down[pos_r, pos_c], preferred_element_type=jnp.float32)
            coarse_pre = term if coarse_pre is None else coarse_pre + term
    coarse_pre = coarse_pre.reshape(half_r, half_c, wide)
    coarse = jax.nn.silu(coarse_pre).astype(jnp.bfloat16)
    upsampled = jnp.einsum(
        "mnc,pqco->mpnqo", coarse, w_up, preferred_element_type=jnp.float32
    ).reshape(rows, cols, width)
    output = (fine.astype(jnp.float32) + upsampled).astype(jnp.bfloat16)
    cot_r = cotangent.reshape(half_r, 2, half_c, 2, width)
    grad_coarse = jnp.einsum("mpnqo,pqco->mnc", cot_r, w_up, preferred_element_type=jnp.float32)
    up_local = jnp.einsum("mnc,mpnqo->pqco", coarse, cot_r, preferred_element_type=jnp.float32)
    grad_cpre = (grad_coarse * silu_slope(coarse_pre)).astype(jnp.bfloat16)
    below = from_behind(grad_cpre[:1], "row", -1)
    grad_rows = jnp.concatenate([grad_cpre, below], axis=0)
    right = from_behind(grad_rows[:, :1], "col", -1)
    grad_ext = jnp.concatenate([grad_rows, right], axis=1)
    phase_of = (1, 0, 1)
    offset_of = (1, 0, 0)
    phases = {}
    grad_flat = grad_cpre.reshape(-1, wide)
    down_parts = []
    for pos_r in range(3):
        for pos_c in range(3):
            start_r = offset_of[pos_r]
            start_c = offset_of[pos_c]
            window = grad_ext[start_r : start_r + half_r, start_c : start_c + half_c].reshape(
                -1, wide
            )
            term = lax.dot_general(
                window,
                w_down[pos_r, pos_c],
                (((1,), (1,)), ((), ())),
                preferred_element_type=jnp.float32,
            )
            slot = (phase_of[pos_r], phase_of[pos_c])
            phases[slot] = term if slot not in phases else phases[slot] + term
            down_parts.append(
                lax.dot_general(
                    strided[pos_r, pos_c],
                    grad_flat,
                    (((0,), (0,)), ((), ())),
                    preferred_element_type=jnp.float32,
                )
            )
    down_local = jnp.stack(down_parts).reshape(3, 3, width, wide)
    even_rows = jnp.stack(
        [phases[0, 0].reshape(half_r, half_c, width), phases[0, 1].reshape(half_r, half_c, width)],
        axis=2,
    )
    odd_rows = jnp.stack(
        [phases[1, 0].reshape(half_r, half_c, width), phases[1, 1].reshape(half_r, half_c, width)],
        axis=2,
    )
    spread = jnp.stack([even_rows, odd_rows], axis=1).reshape(rows, cols, width)
    grad_fine = cotangent.astype(jnp.float32) + spread
    grad_pre = (grad_fine * silu_slope(pre)).astype(jnp.bfloat16)
    grad_pad = extended(grad_pre, (("row", 0), ("col", 1)), 1)
    grad_x = None
    conv_parts = []
    grad_pre_flat = grad_pre.reshape(-1, width)
    for pos_r in range(3):
        for pos_c in range(3):
            window = grad_pad[2 - pos_r : 2 - pos_r + rows, 2 - pos_c : 2 - pos_c + cols].reshape(
                -1, width
            )
            term = lax.dot_general(
                window,
                w_conv[pos_r, pos_c],
                (((1,), (1,)), ((), ())),
                preferred_element_type=jnp.float32,
            )
            grad_x = term if grad_x is None else grad_x + term
            source = padded[pos_r : pos_r + rows, pos_c : pos_c + cols].reshape(-1, width)
            conv_parts.append(
                lax.dot_general(
                    source,
                    grad_pre_flat,
                    (((0,), (0,)), ((), ())),
                    preferred_element_type=jnp.float32,
                )
            )
    grad_inputs = grad_x.reshape(rows, cols, width).astype(jnp.bfloat16)
    conv_local = jnp.stack(conv_parts).reshape(-1)
    conv_sum, down_sum, up_sum = (
        lax.psum_scatter(conv_local, ("row", "col"), scatter_dimension=0, tiled=True),
        lax.psum_scatter(down_local.reshape(-1), ("row", "col"), scatter_dimension=0, tiled=True),
        lax.psum_scatter(up_local.reshape(-1), ("row", "col"), scatter_dimension=0, tiled=True),
    )
    scale = 1.0 / math.sqrt(rows * n_row * cols * n_col)
    return (output, grad_inputs, conv_sum * scale, down_sum * scale, up_sum * scale)


def solution(mesh):
    return jax.shard_map(
        body,
        mesh=mesh,
        in_specs=(P("row", "col", None), P("row", "col", None), P(), P(), P()),
        out_specs=(
            P("row", "col", None),
            P("row", "col", None),
            P(("row", "col")),
            P(("row", "col")),
            P(("row", "col")),
        ),
        check_vma=False,
    )
```

profile of v0, /device:TPU:0, one launch (start us, length us, event | category | flops | bytes accessed | tf_op | source)
XLA Modules:
  0.0 287.4 jit_solution(755731116963576894)
XLA Ops:
  8.0 4.8 %collective-permute-start = (bf16[1,56,128]{2,1,0:T(8,128)(2,1)S(1)}, bf16[1,56,128]{2,1,0:T(8,128)(2,1)S(1)}, u32[]{:S(2)}, u32[]{:S(2)}) collective-permute-start(bf16[1,56,128]{2,1,0:T(8,128)(2,1)S(1)} %get-tuple-element.37), channel_id=1, source_target_pairs={{0,8},{8,16},{16,24},{1,9},{9,17},{17,25},{2,10},{10,18},{18,26},{... | collective-permute-start | bytes 43016 | tf_op jit(solution)/shard_map/ppermute | solution.py:14
  15.5 2.9 %collective-permute-done.1 = bf16[1,56,128]{2,1,0:T(8,128)(2,1)S(1)} collective-permute-done((bf16[1,56,128]{2,1,0:T(8,128)(2,1)S(1)}, bf16[1,56,128]{2,1,0:T(8,128)(2,1)S(1)}, u32[]{:S(2)}, u32[]{:S(2)}) %collective-permute-start.1) | collective-permute-done | bytes 14368 | tf_op jit(solution)/shard_map/ppermute | solution.py:17
  21.7 2.9 %collective-permute-done.3 = bf16[34,1,128]{2,1,0:T(2,128)(2,1)S(1)} collective-permute-done((bf16[34,1,128]{2,1,0:T(2,128)(2,1)S(1)}, bf16[34,1,128]{2,1,0:T(2,128)(2,1)S(1)}, u32[]{:S(2)}, u32[]{:S(2)}) %collective-permute-start.3) | collective-permute-done | bytes 8736 | tf_op jit(solution)/shard_map/ppermute | solution.py:17
  28.7 4.3 %collective-permute-start.4 = (bf16[1,56,128]{2,1,0:T(8,128)(2,1)S(1)}, bf16[1,56,128]{2,1,0:T(8,128)(2,1)S(1)}, u32[]{:S(2)}, u32[]{:S(2)}) collective-permute-start(bf16[1,56,128]{2,1,0:T(8,128)(2,1)S(1)} %slice.288), channel_id=1, source_target_pairs={{0,8},{8,16},{16,24},{1,9},{9,17},{17,25},{2,10},{10,18},{18,26},{... | collective-permute-start | bytes 43016 | tf_op jit(solution)/shard_map/ppermute | solution.py:25
  39.2 4.7 %collective-permute-start.5 = (bf16[33,1,128]{2,1,0:T(2,128)(2,1)}, bf16[33,1,128]{2,1,0:T(2,128)(2,1)}, u32[]{:S(2)}, u32[]{:S(2)}) collective-permute-start(bf16[33,1,128]{2,1,0:T(2,128)(2,1)} %fusion.116), channel_id=1, source_target_pairs={{0,1},{1,2},{2,3},{3,4},{4,5},{5,6},{6,7},{8,9},{9,10},{10,11},{11... | collective-permute-start | bytes 25352 | tf_op jit(solution)/shard_map/ppermute | solution.py:25
  44.7 6.2 %slice.243 = bf16[16,28,128]{2,1,0:T(8,128)(2,1)S(1)} slice(bf16[33,56,128]{2,1,0:T(8,128)(2,1)} %pad_maximum_fusion.1), slice={[0:31:2], [0:55:2], [0:128:1]} | slice | bytes 229376 | tf_op jit(solution)/shard_map/slice | solution.py:63
  53.3 8.2 %slice.245 = bf16[16,28,128]{2,1,0:T(8,128)(2,1)} slice(bf16[33,56,128]{2,1,0:T(8,128)(2,1)} %pad_maximum_fusion.1), slice={[0:31:2], [1:56:2], [0:128:1]} | slice | bytes 229376 | tf_op jit(solution)/shard_map/slice | solution.py:63
  62.4 1.7 maximum_maximum_fusion.1
  64.1 6.2 %slice.241 = bf16[16,28,128]{2,1,0:T(8,128)(2,1)S(1)} slice(bf16[33,57,128]{2,1,0:T(8,128)(2,1)} %maximum_maximum_fusion.1), slice={[0:31:2], [0:55:2], [0:128:1]} | slice | bytes 229376 | tf_op jit(solution)/shard_map/slice | solution.py:63
  70.3 6.3 %slice.247 = bf16[16,28,128]{2,1,0:T(8,128)(2,1)S(1)} slice(bf16[33,57,128]{2,1,0:T(8,128)(2,1)} %maximum_maximum_fusion.1), slice={[1:32:2], [0:55:2], [0:128:1]} | slice | bytes 229376 | tf_op jit(solution)/shard_map/slice | solution.py:63
  76.6 6.3 %slice.253 = bf16[16,28,128]{2,1,0:T(8,128)(2,1)S(1)} slice(bf16[33,57,128]{2,1,0:T(8,128)(2,1)} %maximum_maximum_fusion.1), slice={[2:33:2], [0:55:2], [0:128:1]} | slice | bytes 229376 | tf_op jit(solution)/shard_map/slice | solution.py:63
  89.9 1.4 fusion.5
  103.7 1.7 reshape.210
  105.4 2.2 fusion.24
  110.2 2.9 %copy.29 = f32[144,2,8,128]{3,1,2,0:T(2,128)} copy(f32[144,2,8,128]{3,2,1,0:T(8,128)} %bitcast.101) | data formatting | bytes 2359296
  113.2 1.5 collective-permute-start.7
  120.9 1.7 stack_reshape.12
  130.7 4.5 %collective-permute-start.8 = (bf16[1,56,128]{2,1,0:T(8,128)(2,1)S(1)}, bf16[1,56,128]{2,1,0:T(8,128)(2,1)S(1)}, u32[]{:S(2)}, u32[]{:S(2)}) collective-permute-start(bf16[1,56,128]{2,1,0:T(8,128)(2,1)S(1)} %get-tuple-element.31), channel_id=1, source_target_pairs={{0,8},{8,16},{16,24},{1,9},{9,17},{17,25},{2,10},{10,18},{18,26},{... | collective-permute-start | bytes 43016 | tf_op jit(solution)/shard_map/ppermute | solution.py:14
  137.8 3.1 %collective-permute-done.9 = bf16[1,56,128]{2,1,0:T(8,128)(2,1)S(1)} collective-permute-done((bf16[1,56,128]{2,1,0:T(8,128)(2,1)S(1)}, bf16[1,56,128]{2,1,0:T(8,128)(2,1)S(1)}, u32[]{:S(2)}, u32[]{:S(2)}) %collective-permute-start.9) | collective-permute-done | bytes 14368 | tf_op jit(solution)/shard_map/ppermute | solution.py:17
  142.3 3.0 %collective-permute-start.11 = (bf16[34,1,128]{2,1,0:T(2,128)(2,1)S(1)}, bf16[34,1,128]{2,1,0:T(2,128)(2,1)S(1)}, u32[]{:S(2)}, u32[]{:S(2)}) collective-permute-start(bf16[34,1,128]{2,1,0:T(2,128)(2,1)S(1)} %get-tuple-element.23), channel_id=1, source_target_pairs={{0,1},{1,2},{2,3},{3,4},{4,5},{5,6},{6,7},{8,9},{9,10},{10,11},{11... | collective-permute-start | bytes 26120 | tf_op jit(solution)/shard_map/ppermute | solution.py:14
  149.9 126.5 %all-reduce.6.cloned.1.call-done = (f32[147456]{0:T(1024)}, f32[294912]{0:T(1024)}, f32[131072]{0:T(1024)}) async-done(((f32[147456]{0:T(1024)}, f32[294912]{0:T(1024)}, f32[131072]{0:T(1024)}), (f32[147456]{0:T(1024)}, f32[294912]{0:T(1024)}, f32[131072]{0:T(1024)})) %all-reduce.6.cloned.1.call-update) | async-done | bytes 2293776
  276.4 1.4 dynamic-slice_multiply_fusion
  277.8 1.4 dynamic-slice_multiply_fusion.1
  279.2 1.3 dynamic-slice_multiply_fusion.2
  (221 shorter events, 65.3 us)
Async XLA Ops:
  7.2 82.7 %copy-start = (bf16[2,2,256,128]{3,2,1,0:T(8,128)(2,1)S(1)}, bf16[2,2,256,128]{3,2,1,0:T(8,128)(2,1)}, u32[]{:S(2)}) copy-start(bf16[2,2,256,128]{3,2,1,0:T(8,128)(2,1)} %param.9) | copy-start | bytes 786436
  7.2 269.2 %all-reduce.6.cloned.1.call-start = ((), (), s32[]{:S(2)}) async-start(), calls=%async_computation | async-start | bytes 4587520
  8.0 6.2 %collective-permute-start = (bf16[1,56,128]{2,1,0:T(8,128)(2,1)S(1)}, bf16[1,56,128]{2,1,0:T(8,128)(2,1)S(1)}, u32[]{:S(2)}, u32[]{:S(2)}) collective-permute-start(bf16[1,56,128]{2,1,0:T(8,128)(2,1)S(1)} %get-tuple-element.37), channel_id=1, source_target_pairs={{0,8},{8,16},{16,24},{1,9},{9,17},{17,25},{2,10},{10,18},{18,26},{... | collective-permute-start | bytes 43016 | tf_op jit(solution)/shard_map/ppermute | solution.py:14
  12.8 5.6 %collective-permute-start.1 = (bf16[1,56,128]{2,1,0:T(8,128)(2,1)S(1)}, bf16[1,56,128]{2,1,0:T(8,128)(2,1)S(1)}, u32[]{:S(2)}, u32[]{:S(2)}) collective-permute-start(bf16[1,56,128]{2,1,0:T(8,128)(2,1)S(1)} %get-tuple-element.36), channel_id=1, source_target_pairs={{8,0},{16,8},{24,16},{9,1},{17,9},{25,17},{10,2},{18,10},{26,18},{... | collective-permute-start | bytes 43016 | tf_op jit(solution)/shard_map/ppermute | solution.py:17
  15.5 5.9 %copy-start.39 = (bf16[33,56,128]{2,1,0:T(8,128)(2,1)}, bf16[33,56,128]{2,1,0:T(8,128)(2,1)S(1)}, u32[]{:S(2)}) copy-start(bf16[33,56,128]{2,1,0:T(8,128)(2,1)S(1)} %get-tuple-element.33) | copy-start | bytes 1419268
  15.5 5.7 %copy-start.17 = (bf16[3,3,128,128]{3,2,1,0:T(8,128)(2,1)S(1)}, bf16[3,3,128,128]{3,2,1,0:T(8,128)(2,1)}, u32[]{:S(2)}) copy-start(bf16[3,3,128,128]{3,2,1,0:T(8,128)(2,1)} %param.7) | copy-start | bytes 884740
  18.5 3.2 %collective-permute-start.2 = (bf16[34,1,128]{2,1,0:T(2,128)(2,1)S(1)}, bf16[34,1,128]{2,1,0:T(2,128)(2,1)S(1)}, u32[]{:S(2)}, u32[]{:S(2)}) collective-permute-start(bf16[34,1,128]{2,1,0:T(2,128)(2,1)S(1)} %get-tuple-element.27), channel_id=1, source_target_pairs={{0,1},{1,2},{2,3},{3,4},{4,5},{5,6},{6,7},{8,9},{9,10},{10,11},{11... | collective-permute-start | bytes 26120 | tf_op jit(solution)/shard_map/ppermute | solution.py:14
  19.8 4.9 %collective-permute-start.3 = (bf16[34,1,128]{2,1,0:T(2,128)(2,1)S(1)}, bf16[34,1,128]{2,1,0:T(2,128)(2,1)S(1)}, u32[]{:S(2)}, u32[]{:S(2)}) collective-permute-start(bf16[34,1,128]{2,1,0:T(2,128)(2,1)S(1)} %get-tuple-element.28), channel_id=1, source_target_pairs={{1,0},{2,1},{3,2},{4,3},{5,4},{6,5},{7,6},{9,8},{10,9},{11,10},{12... | collective-permute-start | bytes 26120 | tf_op jit(solution)/shard_map/ppermute | solution.py:17
  28.7 9.8 %collective-permute-start.4 = (bf16[1,56,128]{2,1,0:T(8,128)(2,1)S(1)}, bf16[1,56,128]{2,1,0:T(8,128)(2,1)S(1)}, u32[]{:S(2)}, u32[]{:S(2)}) collective-permute-start(bf16[1,56,128]{2,1,0:T(8,128)(2,1)S(1)} %slice.288), channel_id=1, source_target_pairs={{0,8},{8,16},{16,24},{1,9},{9,17},{17,25},{2,10},{10,18},{18,26},{... | collective-permute-start | bytes 43016 | tf_op jit(solution)/shard_map/ppermute | solution.py:25
  34.1 10.6 %copy-start.22 = (bf16[16,28,128]{2,1,0:T(8,128)(2,1)}, bf16[16,28,128]{2,1,0:T(8,128)(2,1)S(1)}, u32[]{:S(2)}) copy-start(bf16[16,28,128]{2,1,0:T(8,128)(2,1)S(1)} %slice.251) | copy-start | bytes 344068
  35.0 9.7 %copy-start.20 = (bf16[16,28,128]{2,1,0:T(8,128)(2,1)}, bf16[16,28,128]{2,1,0:T(8,128)(2,1)S(1)}, u32[]{:S(2)}) copy-start(bf16[16,28,128]{2,1,0:T(8,128)(2,1)S(1)} %slice.255) | copy-start | bytes 344068
  35.8 8.9 %copy-start.18 = (bf16[16,28,128]{2,1,0:T(8,128)(2,1)}, bf16[16,28,128]{2,1,0:T(8,128)(2,1)S(1)}, u32[]{:S(2)}) copy-start(bf16[16,28,128]{2,1,0:T(8,128)(2,1)S(1)} %slice.257) | copy-start | bytes 344068
  37.2 15.0 %copy-start.2 = (bf16[3,3,128,256]{3,2,1,0:T(8,128)(2,1)S(1)}, bf16[3,3,128,256]{3,2,1,0:T(8,128)(2,1)}, u32[]{:S(2)}) copy-start(bf16[3,3,128,256]{3,2,1,0:T(8,128)(2,1)} %param.8) | copy-start | bytes 1769476
  39.2 23.2 %collective-permute-start.5 = (bf16[33,1,128]{2,1,0:T(2,128)(2,1)}, bf16[33,1,128]{2,1,0:T(2,128)(2,1)}, u32[]{:S(2)}, u32[]{:S(2)}) collective-permute-start(bf16[33,1,128]{2,1,0:T(2,128)(2,1)} %fusion.116), channel_id=1, source_target_pairs={{0,1},{1,2},{2,3},{3,4},{4,5},{5,6},{6,7},{8,9},{9,10},{10,11},{11... | collective-permute-start | bytes 25352 | tf_op jit(solution)/shard_map/ppermute | solution.py:25
  70.3 13.9 %copy-start.33 = (bf16[16,28,128]{2,1,0:T(8,128)(2,1)}, bf16[16,28,128]{2,1,0:T(8,128)(2,1)S(1)}, u32[]{:S(2)}) copy-start(bf16[16,28,128]{2,1,0:T(8,128)(2,1)S(1)} %slice.241) | copy-start | bytes 344068
  76.6 7.7 %copy-start.31 = (bf16[16,28,128]{2,1,0:T(8,128)(2,1)}, bf16[16,28,128]{2,1,0:T(8,128)(2,1)S(1)}, u32[]{:S(2)}) copy-start(bf16[16,28,128]{2,1,0:T(8,128)(2,1)S(1)} %slice.247) | copy-start | bytes 344068
  98.9 6.5 %copy-start.46 = (bf16[32,56,128]{2,1,0:T(8,128)(2,1)S(1)}, bf16[32,56,128]{2,1,0:T(8,128)(2,1)}, u32[]{:S(2)}) copy-start(bf16[32,56,128]{2,1,0:T(8,128)(2,1)} %param.6) | copy-start | bytes 1376260
  102.4 10.7 %collective-permute-start.6 = (bf16[1,28,256]{2,1,0:T(8,128)(2,1)S(1)}, bf16[1,28,256]{2,1,0:T(8,128)(2,1)S(1)}, u32[]{:S(2)}, u32[]{:S(2)}) collective-permute-start(bf16[1,28,256]{2,1,0:T(8,128)(2,1)S(1)} %slice.291), channel_id=1, source_target_pairs={{8,0},{16,8},{24,16},{9,1},{17,9},{25,17},{10,2},{18,10},{26,18},{... | collective-permute-start | bytes 43016 | tf_op jit(solution)/shard_map/ppermute | solution.py:25
  113.2 4.3 %collective-permute-start.7 = (bf16[17,1,256]{2,1,0:T(2,128)(2,1)S(1)}, bf16[17,1,256]{2,1,0:T(2,128)(2,1)S(1)}, u32[]{:S(2)}, u32[]{:S(2)}) collective-permute-start(bf16[17,1,256]{2,1,0:T(2,128)(2,1)S(1)} %pad_maximum_fusion.12), channel_id=1, source_target_pairs={{1,0},{2,1},{3,2},{4,3},{5,4},{6,5},{7,6},{9,8},{10,9},{11,10},{12... | collective-permute-start | bytes 26120 | tf_op jit(solution)/shard_map/ppermute | solution.py:25
  129.7 6.9 %copy-start.4 = (bf16[32,56,128]{2,1,0:T(8,128)(2,1)S(1)}, bf16[32,56,128]{2,1,0:T(8,128)(2,1)}, u32[]{:S(2)}) copy-start(bf16[32,56,128]{2,1,0:T(8,128)(2,1)} %copy-done.3) | copy-start | bytes 1376260
  130.7 7.0 %collective-permute-start.8 = (bf16[1,56,128]{2,1,0:T(8,128)(2,1)S(1)}, bf16[1,56,128]{2,1,0:T(8,128)(2,1)S(1)}, u32[]{:S(2)}, u32[]{:S(2)}) collective-permute-start(bf16[1,56,128]{2,1,0:T(8,128)(2,1)S(1)} %get-tuple-element.31), channel_id=1, source_target_pairs={{0,8},{8,16},{16,24},{1,9},{9,17},{17,25},{2,10},{10,18},{18,26},{... | collective-permute-start | bytes 43016 | tf_op jit(solution)/shard_map/ppermute | solution.py:14
  135.3 5.6 %collective-permute-start.9 = (bf16[1,56,128]{2,1,0:T(8,128)(2,1)S(1)}, bf16[1,56,128]{2,1,0:T(8,128)(2,1)S(1)}, u32[]{:S(2)}, u32[]{:S(2)}) collective-permute-start(bf16[1,56,128]{2,1,0:T(8,128)(2,1)S(1)} %get-tuple-element.32), channel_id=1, source_target_pairs={{8,0},{16,8},{24,16},{9,1},{17,9},{25,17},{10,2},{18,10},{26,18},{... | collective-permute-start | bytes 43016 | tf_op jit(solution)/shard_map/ppermute | solution.py:17
  141.0 4.7 %collective-permute-start.10 = (bf16[34,1,128]{2,1,0:T(2,128)(2,1)S(1)}, bf16[34,1,128]{2,1,0:T(2,128)(2,1)S(1)}, u32[]{:S(2)}, u32[]{:S(2)}) collective-permute-start(bf16[34,1,128]{2,1,0:T(2,128)(2,1)S(1)} %get-tuple-element.22), channel_id=1, source_target_pairs={{1,0},{2,1},{3,2},{4,3},{5,4},{6,5},{7,6},{9,8},{10,9},{11,10},{12... | collective-permute-start | bytes 26120 | tf_op jit(solution)/shard_map/ppermute | solution.py:17
  142.3 3.9 %collective-permute-start.11 = (bf16[34,1,128]{2,1,0:T(2,128)(2,1)S(1)}, bf16[34,1,128]{2,1,0:T(2,128)(2,1)S(1)}, u32[]{:S(2)}, u32[]{:S(2)}) collective-permute-start(bf16[34,1,128]{2,1,0:T(2,128)(2,1)S(1)} %get-tuple-element.23), channel_id=1, source_target_pairs={{0,1},{1,2},{2,3},{3,4},{4,5},{5,6},{6,7},{8,9},{9,10},{10,11},{11... | collective-permute-start | bytes 26120 | tf_op jit(solution)/shard_map/ppermute | solution.py:14
  (39 other events, 74.0 us)
Sparse Core Ops, SparseCore 0:
  137.9 138.4 all-reduce.5
where the time goes:
time: 292 us; the launch traced here: 287 us
  waiting for transfers between devices  136 us (47%)
  local copies, waits for them, and re-layouts  60.4 us (21%)
  matrix products  34.2 us (12%)
  starting transfers between devices  30.6 us (10%)
  between operations  15 us (5%)
  other arithmetic  11.1 us (4%)
    unnamed x2, waiting for transfers between devices  126 us
    slice x9, local copies, waits for them, and re-layouts, body(): fine_ext[pos_r:pos_r + 2 * half_r - 1:2, pos_c:pos_c + 2 * half_c - 1:2]  35.8 us
    ppermute x4, starting transfers between devices, extended(): lax.ppermute(lax.slice_in_dim(block, block.shape[dim] - width, None, axis...  13.7 us
    ppermute x4, starting transfers between devices, from_behind(): lax.ppermute(value, axis, [(source, source + steps) for source in range(l...  11.7 us
    unnamed x102, local copies, waits for them, and re-layouts  9.14 us
    ppermute x4, waiting for transfers between devices, extended(): lax.ppermute(lax.slice_in_dim(block, 0, width, axis=dim), axis, backward)  9 us
    dot_general x9, matrix products, body(): lax.dot_general(window, w_down[pos_r, pos_c], (((1,), (1,)), ((), ())), p...  8.38 us
    dot_general x9, matrix products, body(): lax.dot_general(strided[pos_r, pos_c], grad_flat, (((0,), (0,)), ((), ())...  7.93 us
  transfers between devices with their start and end apart: 13, of which 6 were waited for; matrix products, arithmetic and copies ran while one was open for 15% of the time, Pallas kernels for 0%

commit v1 on v0

v1 whole, which is shorter than its diff:
```python
import functools
import math

import jax
import jax.numpy as jnp
from jax import lax
from jax.experimental import pallas as pl
from jax.experimental.pallas import tpu as pltpu
from jax.sharding import PartitionSpec as P

MESH = pl.DeviceIdType.MESH
F32 = jnp.float32
BF16 = jnp.bfloat16
VMEM = pl.BlockSpec(memory_space=pltpu.VMEM)
NT = (((1,), (1,)), ((), ()))
TN = (((0,), (0,)), ((), ()))
SHIFTS = [(dr, dc) for dr in (-1, 0, 1) for dc in (-1, 0, 1) if (dr, dc) != (0, 0)]


def dot(a, b):
    return jnp.dot(a, b, preferred_element_type=F32)


def dot_nt(a, b):
    return lax.dot_general(a, b, NT, preferred_element_type=F32)


def dot_tn(a, b):
    return lax.dot_general(a, b, TN, preferred_element_type=F32)


def halo_kernel(n_row, n_col, x_ref, ct_ref, *rest):
    outs, (pack, send_sem, recv_sem) = rest[:10], rest[10:]
    x_top, x_bot, ct_top, ct_bot, left, right, tl, tr, bl, br = outs
    rows, cols, _ = x_ref.shape
    r, c = lax.axis_index("row"), lax.axis_index("col")

    def exists(dr, dc):
        ok = None
        for d, at, n in ((dr, r, n_row), (dc, c, n_col)):
            if d:
                here = at > 0 if d < 0 else at < n - 1
                ok = here if ok is None else jnp.logical_and(ok, here)
        return ok

    barrier = pltpu.get_barrier_semaphore()
    for dr, dc in SHIFTS:

        @pl.when(exists(dr, dc))
        def _(dr=dr, dc=dc):
            pl.semaphore_signal(barrier, inc=1, device_id=(r + dr, c + dc), device_id_type=MESH)

    pack[0] = jnp.concatenate(
        [x_ref[:, 0:8, :].astype(F32), ct_ref[:, 0:8, :].astype(F32)], axis=1
    ).astype(BF16)
    pack[1] = jnp.concatenate(
        [x_ref[:, cols - 8 : cols, :].astype(F32), ct_ref[:, cols - 8 : cols, :].astype(F32)],
        axis=1,
    ).astype(BF16)
    near_r = 3 - (r == 0).astype(jnp.int32) - (r == n_row - 1).astype(jnp.int32)
    near_c = 3 - (c == 0).astype(jnp.int32) - (c == n_col - 1).astype(jnp.int32)
    pl.semaphore_wait(barrier, near_r * near_c - 1)

    low, high = pl.ds(0, 4), pl.ds(rows - 4, 4)
    plan = [
        ((1, 0), x_ref.at[high], x_top),
        ((-1, 0), x_ref.at[low], x_bot),
        ((1, 0), ct_ref.at[high], ct_top),
        ((-1, 0), ct_ref.at[low], ct_bot),
        ((0, 1), pack.at[1], left),
        ((0, -1), pack.at[0], right),
        ((1, 1), pack.at[1, high], tl),
        ((1, -1), pack.at[0, high], tr),
        ((-1, 1), pack.at[1, low], bl),
        ((-1, -1), pack.at[0, low], br),
    ]

    def copy(k):
        (dr, dc), src, dst = plan[k]
        return pltpu.make_async_remote_copy(
            src_ref=src,
            dst_ref=dst,
            send_sem=send_sem.at[k],
            recv_sem=recv_sem.at[k],
            device_id=(r + dr, c + dc),
            device_id_type=MESH,
        )

    for k, ((dr, dc), _, _) in enumerate(plan):

        @pl.when(exists(dr, dc))
        def _(k=k):
            copy(k).start()

    for k, ((dr, dc), _, _) in enumerate(plan):

        @pl.when(exists(dr, dc))
        def _(k=k):
            copy(k).wait_send()

        @pl.when(exists(-dr, -dc))
        def _(k=k):
            copy(k).wait_recv()


def halos(n_row, n_col, x, ct):
    rows, cols, width = x.shape
    shapes = [(4, cols, width)] * 4 + [(rows, 16, width)] * 2 + [(4, 16, width)] * 4
    return pl.pallas_call(
        functools.partial(halo_kernel, n_row, n_col),
        out_shape=[jax.ShapeDtypeStruct(s, BF16) for s in shapes],
        in_specs=[VMEM] * 2,
        out_specs=[VMEM] * 10,
        scratch_shapes=[
            pltpu.VMEM((2, rows, 16, width), BF16),
            pltpu.SemaphoreType.DMA((10,)),
            pltpu.SemaphoreType.DMA((10,)),
        ],
        compiler_params=pltpu.CompilerParams(
            collective_id=0, has_side_effects=True, vmem_limit_bytes=32 * 2**20
        ),
        name="halos",
    )(x, ct)


def level_kernel(n_row, n_col, *refs):
    (x_ref, ct_ref, x_top, x_bot, ct_top, ct_bot, left, right, tl, tr, bl, br, wc, wd, wu) = refs[:15]
    (out_ref, gx_ref, conv_sum, down_sum, up_sum) = refs[15:20]
    (xf, x3, ce, fine, slope, d3, t4, cp, co, g, gp, g3, up) = refs[20:]
    rows, cols, ch = x_ref.shape
    wide = wd.shape[3]
    r, c = lax.axis_index("row"), lax.axis_index("col")
    has_top, has_bot = r > 0, r < n_row - 1
    has_left, has_right = c > 0, c < n_col - 1
    ce_rows, a_rows, u_rows = rows + 4, rows + 6, rows // 2 + 2
    half = rows // 2

    def assemble(dst, offset, at, own, lft, rgt, row_ok):
        n = own.shape[0]
        ok_l, ok_r = has_left, has_right
        if row_ok is not None:
            own = jnp.where(row_ok, own.astype(F32), 0.0)
            ok_l = jnp.logical_and(ok_l, row_ok)
            ok_r = jnp.logical_and(ok_r, row_ok)
        rows_at = pl.ds(at, n)
        dst[rows_at, 0:offset, :] = jnp.where(ok_l, lft.astype(F32), 0.0)[:, 8 - offset : 8, :]
        dst[rows_at, offset : offset + cols, :] = own.astype(F32)
        dst[rows_at, offset + cols : offset + cols + 8, :] = jnp.where(ok_r, rgt.astype(F32), 0.0)

    xs, cs = slice(0, 8), slice(8, 16)
    xf[:, 64:72, :] = jnp.zeros((rows + 8, 8, ch), F32)
    ce[:, 64:72, :] = jnp.zeros((ce_rows, 8, ch), F32)
    assemble(xf, 4, 0, x_top[...], tl[:, xs, :], tr[:, xs, :], has_top)
    assemble(xf, 4, rows + 4, x_bot[...], bl[:, xs, :], br[:, xs, :], has_bot)
    assemble(ce, 3, 0, ct_top[2:4], tl[2:4, cs, :], tr[2:4, cs, :], has_top)
    assemble(ce, 3, rows + 2, ct_bot[0:2], bl[0:2, cs, :], br[0:2, cs, :], has_bot)

    @pl.loop(0, rows // 8)
    def _(k):
        at = pl.ds(k * 8, 8)
        assemble(xf, 4, 4 + k * 8, x_ref[at], left[at, xs, :], right[at, xs, :], None)
        assemble(ce, 3, 2 + k * 8, ct_ref[at], left[at, cs, :], right[at, cs, :], None)

    @pl.loop(0, (rows + 8) // 4)
    def _(k):
        at = pl.ds(k * 4, 4)
        for q in range(3):
            x3[at, :, q * ch : (q + 1) * ch] = xf[at, q : q + 64, :].astype(BF16)

    wc_rows = wc[...].reshape(3, 3 * ch, ch)
    j_at = lax.broadcasted_iota(jnp.int32, (1, 64, 1), 1) - 3
    col_ok = jnp.logical_and(
        jnp.logical_or(j_at >= 0, has_left), jnp.logical_or(j_at < cols, has_right)
    )
    fine[:, 64:72, :] = jnp.zeros((a_rows, 8, ch), F32)
    slope[:, 64:72, :] = jnp.zeros((a_rows, 8, ch), F32)
    gp[:, 64:72, :] = jnp.zeros((a_rows, 8, ch), F32)

    def in_grid(first, n):
        i_at = lax.broadcasted_iota(jnp.int32, (n, 1, 1), 0) + (first - 3)
        row_ok = jnp.logical_and(
            jnp.logical_or(i_at >= 0, has_top), jnp.logical_or(i_at < rows, has_bot)
        )
        return jnp.logical_and(row_ok, col_ok)

    step = a_rows // 2

    @pl.loop(0, 2)
    def _(k):
        pre = None
        for p in range(3):
            term = dot(x3[pl.ds(k * step + p, step)].reshape(step * 64, 3 * ch), wc_rows[p])
            pre = term if pre is None else pre + term
        sig = jax.nn.sigmoid(pre)
        at = pl.ds(k * step, step)
        ok = in_grid(k * step, step)
        value = (pre * sig).reshape(step, 64, ch)
        fine[at, 0:64, :] = jnp.where(ok, value, 0.0)
        slope[at, 0:64, :] = (sig * (1.0 + pre * (1.0 - sig))).reshape(step, 64, ch)

    @pl.loop(0, a_rows // 2)
    def _(k):
        for p in range(2):
            for q in range(3):
                d3[k, p, :, q * ch : (q + 1) * ch] = fine[
                    2 * k + p, pl.ds(q, 32, stride=2), :
                ].astype(BF16)

    @pl.loop(0, u_rows)
    def _(k):
        for p in range(2):
            for q in range(2):
                e = 2 * p + q
                t4[k, :, e * ch : (e + 1) * ch] = ce[
                    2 * k + p, pl.ds(1 + q, 32, stride=2), :
                ].astype(BF16)

    wd_rows = wd[...].reshape(3, 3 * ch, wide)
    cpre = None
    for p in range(3):
        window = d3[p // 2 : p // 2 + u_rows, p % 2].reshape(u_rows * 32, 3 * ch)
        term = dot(window, wd_rows[p])
        cpre = term if cpre is None else cpre + term
    cp[...] = cpre.reshape(u_rows, 32, wide)
    v_at = lax.broadcasted_iota(jnp.int32, (1, 32, 1), 1) - 1
    v_own = jnp.logical_and(v_at >= 0, v_at < cols // 2)
    sig = jax.nn.sigmoid(cp[...])
    co[...] = (cp[...] * sig).astype(BF16)
    grad = None
    for e in range(4):
        term = dot_nt(
            t4[:, :, e * ch : (e + 1) * ch].reshape(u_rows * 32, ch), wu[e // 2, e % 2]
        )
        grad = term if grad is None else grad + term
    u_at = lax.broadcasted_iota(jnp.int32, (u_rows, 1, 1), 0) - 1
    ok = jnp.logical_and(
        jnp.logical_and(jnp.logical_or(u_at >= 0, has_top), jnp.logical_or(u_at < half, has_bot)),
        jnp.logical_and(
            jnp.logical_or(v_at >= 0, has_left), jnp.logical_or(v_at < cols // 2, has_right)
        ),
    )
    full = cp[...]
    sig = jax.nn.sigmoid(full)
    part = grad.reshape(u_rows, 32, wide) * (sig * (1.0 + full * (1.0 - sig)))
    g[:, 32:40, :] = jnp.zeros((u_rows, 8, wide), F32)
    g[:, 0:32, :] = jnp.where(ok, part, 0.0)

    co_rows = co[1 : half + 1].reshape(half * 32, wide)
    for e in range(4):
        p, q = e // 2, e % 2
        res = dot(co_rows, wu[p, q]).reshape(half, 32, ch)
        for m in range(half):
            up[2 * m + p, pl.ds(1 + q, 32, stride=2), :] = res[m]

    @pl.loop(0, rows // 4)
    def _(k):
        f = fine[pl.ds(3 + k * 4, 4), 3 : 3 + cols, :].astype(BF16).astype(F32)
        out_ref[pl.ds(k * 4, 4)] = (f + up[pl.ds(k * 4, 4), 3 : 3 + cols, :]).astype(BF16)

    own_co = jnp.where(v_own, co[1 : half + 1].astype(F32), 0.0).astype(BF16)
    us = dot_tn(own_co.reshape(half * 32, wide), t4[1 : half + 1].reshape(half * 32, 4 * ch))
    for e in range(4):
        up_sum[e * wide : (e + 1) * wide, :] = us[:, e * ch : (e + 1) * ch]
    own_g = jnp.where(v_own, g[1 : half + 1, 0:32, :], 0.0).astype(BF16).reshape(half * 32, wide)
    for p in range(3):
        window = d3[p // 2 + 1 : p // 2 + 1 + half, p % 2].reshape(half * 32, 3 * ch)
        down_sum[p * 3 * ch : (p + 1) * 3 * ch, :] = dot_tn(window, own_g)

    g_here = g[:, 0:32, :].astype(BF16).reshape(u_rows * 32, wide)
    g_next = g[:, 1:33, :].astype(BF16).reshape(u_rows * 32, wide)
    less = (u_rows - 1) * 32

    def pair(p):
        return jnp.concatenate([wd[p, 1], wd[p, 2]], axis=0)

    even = dot_nt(g_here, pair(1))
    even_odd = even[:, ch:] + dot_nt(g_next, wd[1, 0])
    odd = dot_nt(g_here[32:], pair(0)) + dot_nt(g_here[:less], pair(2))
    odd_odd = odd[:, ch:] + dot_nt(g_next[32:], wd[0, 0]) + dot_nt(g_next[:less], wd[2, 0])
    spread = {
        (0, 0): even[:, :ch],
        (0, 1): even_odd,
        (1, 0): odd[:, :ch],
        (1, 1): odd_odd,
    }
    for (s, t), value in spread.items():
        for u in range(u_rows - s):
            at = pl.ds(1 + t, 32, stride=2)
            ce[2 * u + s, at, :] = ce[2 * u + s, at, :] + value[u * 32 : (u + 1) * 32]

    @pl.loop(0, (rows + 2) // 2)
    def _(k):
        a = 2 + 2 * k
        value = ce[pl.ds(a - 1, 2), 0:64, :] * slope[pl.ds(a, 2), 0:64, :]
        gp[pl.ds(a, 2), 0:64, :] = jnp.where(in_grid(a, 2), value, 0.0)

    @pl.loop(0, (rows + 2) // 2)
    def _(k):
        at = pl.ds(2 + 2 * k, 2)
        for q in range(3):
            g3[at, :, q * ch : (q + 1) * ch] = gp[at, 4 - q : 68 - q, :].astype(BF16)

    j_own = jnp.logical_and(j_at >= 0, j_at < cols)
    own = jnp.where(j_own, gp[3 : rows + 3, 0:64, :], 0.0).astype(BF16)

    def shift(p):
        pieces = [own]
        if p > 0:
            pieces.insert(0, jnp.zeros((p, 64, ch), BF16))
        if p < 2:
            pieces.append(jnp.zeros((2 - p, 64, ch), BF16))
        return jnp.concatenate(pieces, axis=0).reshape((rows + 2) * 64, ch)

    shifted = [shift(p) for p in range(3)]
    sums = dot_tn(
        x3[3 : rows + 5].reshape((rows + 2) * 64, 3 * ch), jnp.concatenate(shifted, axis=1)
    )
    for p in range(3):
        conv_sum[p * 3 * ch : (p + 1) * 3 * ch, :] = sums[:, p * ch : (p + 1) * ch]

    turned = [jnp.concatenate([wc[p, q] for q in range(3)], axis=1) for p in range(3)]
    part_rows = rows // 2

    @pl.loop(0, 2)
    def _(k):
        total = None
        for p in range(3):
            window = g3[pl.ds(k * part_rows + 4 - p, part_rows)].reshape(part_rows * 64, 3 * ch)
            term = dot_nt(window, turned[p])
            total = term if total is None else total + term
        total = total.reshape(part_rows, 64, ch)[:, :cols, :]
        gx_ref[pl.ds(k * part_rows, part_rows)] = total.astype(BF16)


def level(n_row, n_col, x, ct, edges, wc, wd, wu):
    rows, cols, ch = x.shape
    wide = wd.shape[3]
    a_rows, u_rows = rows + 6, rows // 2 + 2
    return pl.pallas_call(
        functools.partial(level_kernel, n_row, n_col),
        out_shape=[
            jax.ShapeDtypeStruct(x.shape, BF16),
            jax.ShapeDtypeStruct(x.shape, BF16),
            jax.ShapeDtypeStruct((9 * ch, ch), F32),
            jax.ShapeDtypeStruct((9 * ch, wide), F32),
            jax.ShapeDtypeStruct((4 * wide, ch), F32),
        ],
        in_specs=[VMEM] * 15,
        out_specs=[VMEM] * 5,
        scratch_shapes=[
            pltpu.VMEM((rows + 8, 72, ch), F32),
            pltpu.VMEM((rows + 8, 64, 3 * ch), BF16),
            pltpu.VMEM((rows + 4, 72, ch), F32),
            pltpu.VMEM((a_rows, 72, ch), F32),
            pltpu.VMEM((a_rows, 72, ch), F32),
            pltpu.VMEM((a_rows // 2, 2, 32, 3 * ch), BF16),
            pltpu.VMEM((u_rows, 32, 4 * ch), BF16),
            pltpu.VMEM((u_rows, 32, wide), F32),
            pltpu.VMEM((u_rows, 32, wide), BF16),
            pltpu.VMEM((u_rows, 40, wide), F32),
            pltpu.VMEM((a_rows, 72, ch), F32),
            pltpu.VMEM((a_rows, 64, 3 * ch), BF16),
            pltpu.VMEM((rows, 72, ch), F32),
        ],
        compiler_params=pltpu.CompilerParams(vmem_limit_bytes=56 * 2**20),
        name="level",
    )(x, ct, *edges, wc, wd, wu)


def sum_kernel(n_row, n_col, scale, conv, down, up, conv_out, down_out, up_out, *rest):
    stage, recv0, acc1, recv1, acc2, recv2, send_sem, recv_sem = rest
    nz = n_col // 2
    blocks = n_row * n_col
    nc, nd, nu = conv.shape[0] // blocks, down.shape[0] // blocks, up.shape[0] // blocks
    r, c = lax.axis_index("row"), lax.axis_index("col")
    z, core = c // 2, c % 2
    peers = [(r, z * 2 + 1 - core)]
    peers += [((r + k) % n_row, c) for k in range(1, n_row)]
    peers += [(r, ((z + k) % nz) * 2 + core) for k in range(1, nz)]
    barrier = pltpu.get_barrier_semaphore()
    for peer in peers:
        pl.semaphore_signal(barrier, inc=1, device_id=peer, device_id_type=MESH)
    pad = stage.shape[1] - nu - 2 * nd - nc
    for row in range(n_row):
        for col in range(n_col):
            d = row * n_col + col
            slot = (col % 2) * (n_row * nz) + row * nz + col // 2
            pieces = [
                up[d * nu : (d + 1) * nu, :],
                down[d * nd : (d + 1) * nd, 0:128],
                down[d * nd : (d + 1) * nd, 128:256],
                conv[d * nc : (d + 1) * nc, :],
                jnp.zeros((pad, 128), F32),
            ]
            stage[slot] = jnp.concatenate(pieces, axis=0).astype(BF16)
    pl.semaphore_wait(barrier, len(peers))

    def copy(k, src, dst):
        return pltpu.make_async_remote_copy(
            src_ref=src,
            dst_ref=dst,
            send_sem=send_sem.at[k],
            recv_sem=recv_sem.at[k],
            device_id=peers[k],
            device_id_type=MESH,
        )

    per_core = n_row * nz
    first = copy(0, stage.at[pl.ds((1 - core) * per_core, per_core)], recv0)
    first.start()
    first.wait()
    for k in range(per_core):
        own = stage[core * per_core + k].astype(F32)
        acc1[k // nz, k % nz] = (own + recv0[k].astype(F32)).astype(BF16)
    copies = [copy(k, acc1.at[(r + k) % n_row], recv1.at[k - 1]) for k in range(1, n_row)]
    for item in copies:
        item.start()
    for item in copies:
        item.wait()
    for k in range(nz):
        total = acc1[r, k].astype(F32)
        for m in range(n_row - 1):
            total = total + recv1[m, k].astype(F32)
        acc2[k] = total.astype(BF16)
    copies = [
        copy(n_row - 1 + k, acc2.at[(z + k) % nz], recv2.at[k - 1]) for k in range(1, nz)
    ]
    for item in copies:
        item.start()
    for item in copies:
        item.wait()
    total = acc2[z].astype(F32)
    for m in range(nz - 1):
        total = total + recv2[m].astype(F32)
    total = total * scale
    up_out[...] = total[0:nu]
    down_out[:, 0:128] = total[nu : nu + nd]
    down_out[:, 128:256] = total[nu + nd : nu + 2 * nd]
    conv_out[...] = total[nu + 2 * nd : nu + 2 * nd + nc]


def scattered(n_row, n_col, scale, conv, down, up):
    blocks, nz = n_row * n_col, n_col // 2
    sizes = [a.shape[0] // blocks for a in (conv, down, up)]
    height = -(-(sizes[0] + 2 * sizes[1] + sizes[2]) // 16) * 16
    return pl.pallas_call(
        functools.partial(sum_kernel, n_row, n_col, scale),
        out_shape=[
            jax.ShapeDtypeStruct((n, a.shape[1]), F32)
            for n, a in zip(sizes, (conv, down, up))
        ],
        in_specs=[VMEM] * 3,
        out_specs=[VMEM] * 3,
        scratch_shapes=[
            pltpu.VMEM((blocks, height, 128), BF16),
            pltpu.VMEM((n_row * nz, height, 128), BF16),
            pltpu.VMEM((n_row, nz, height, 128), BF16),
            pltpu.VMEM((n_row - 1, nz, height, 128), BF16),
            pltpu.VMEM((nz, height, 128), BF16),
            pltpu.VMEM((nz - 1, height, 128), BF16),
            pltpu.SemaphoreType.DMA((n_row + nz - 1,)),
            pltpu.SemaphoreType.DMA((n_row + nz - 1,)),
        ],
        compiler_params=pltpu.CompilerParams(
            collective_id=1, has_side_effects=True, vmem_limit_bytes=48 * 2**20
        ),
        name="sums",
    )(conv, down, up)


def body(n_row, n_col, inputs, cotangent, w_conv, w_down, w_up):
    rows, cols, _ = inputs.shape
    edges = halos(n_row, n_col, inputs, cotangent)
    output, grad_inputs, *sums = level(
        n_row, n_col, inputs, cotangent, edges, w_conv, w_down, w_up
    )
    scale = 1.0 / math.sqrt(rows * n_row * cols * n_col)
    blocks = n_row * n_col
    if all(a.shape[0] % blocks == 0 for a in sums):
        sums = scattered(n_row, n_col, scale, *sums)
        return (output, grad_inputs, *(a.reshape(-1) for a in sums))
    sums = [
        lax.psum_scatter(a.reshape(-1), ("row", "col"), scatter_dimension=0, tiled=True) * scale
        for a in sums
    ]
    return (output, grad_inputs, *sums)


def solution(mesh):
    return jax.shard_map(
        functools.partial(body, mesh.shape["row"], mesh.shape["col"]),
        mesh=mesh,
        in_specs=(P("row", "col", None), P("row", "col", None), P(), P(), P()),
        out_specs=(
            P("row", "col", None),
            P("row", "col", None),
            P(("row", "col")),
            P(("row", "col")),
            P(("row", "col")),
        ),
        check_vma=False,
    )
```

time: 292 us -> 56.8 us (0.19); the launches traced: 287 us -> 56.5 us
  waiting for transfers between devices: 136 us -> 0 us
  local copies, waits for them, and re-layouts: 60.4 us -> 13.4 us
  Pallas kernels: 0 us -> 42.4 us
  matrix products: 34.2 us -> 0 us
  starting transfers between devices: 30.6 us -> 0 us
  between operations: 15 us -> 0.68 us
  other arithmetic: 11.1 us -> 0 us
    unnamed x2 -> x0, waiting for transfers between devices: 126 us -> none
    pallas_call x0 -> x3, Pallas kernels: none -> 42.4 us  [the longest x1 18.5 us: scattered(): pl.pallas_call(functools.partial(sum_kernel, n_row, n_col, scale), out_sh...]
    slice x19 -> x0, local copies, waits for them, and re-layouts: 37.2 us -> none  [the longest x9 35.8 us: body(): fine_ext[pos_r:pos_r + 2 * half_r - 1:2, pos_c:pos_c + 2 * half_c - 1:2]]
    dot_general x57 -> x0, matrix products: 34.2 us -> none  [the longest x9 8.38 us: body(): lax.dot_general(window, w_down[pos_r, pos_c], (((1,), (1,)), ((), ())), p...]
    ppermute x12 -> x0, starting transfers between devices: 30.6 us -> none  [the longest x4 13.7 us: extended(): lax.ppermute(lax.slice_in_dim(block, block.shape[dim] - width, None, axis...]
    ppermute x12 -> x0, waiting for transfers between devices: 9.59 us -> none  [the longest x4 9 us: extended(): lax.ppermute(lax.slice_in_dim(block, 0, width, axis=dim), axis, backward)]
    reshape x14 -> x1, local copies, waits for them, and re-layouts: 7.24 us -> 0.62 us  [body(): return (output, grad_inputs, *(a.reshape(-1) for a in sums))]
    mul x3 -> x0, other arithmetic: 4.13 us -> none  [the longest x1 1.42 us: body(): conv_sum * scale]
  transfers between devices with their start and end apart: 13 -> 0, of which waited for: 6 -> 0; matrix products, arithmetic and copies ran while one was open for 15% -> 0% of each run, Pallas kernels for 0% -> 0%
where the time goes in v1:
time: 56.8 us; the launch traced here: 56.5 us
  Pallas kernels  42.4 us (75%)
  local copies, waits for them, and re-layouts  13.4 us (24%)
  between operations  0.68 us (1%)
    pallas_call x1, Pallas kernels, scattered(): pl.pallas_call(functools.partial(sum_kernel, n_row, n_col, scale), out_sh...  18.5 us
    unnamed x32, local copies, waits for them, and re-layouts  12.8 us
    pallas_call x1, Pallas kernels, halos(): pl.pallas_call(functools.partial(halo_kernel, n_row, n_col), out_shape=[j...  12.1 us
    pallas_call x1, Pallas kernels, level(): pl.pallas_call(functools.partial(level_kernel, n_row, n_col), out_shape=[...  11.7 us

profile of v1, /device:TPU:0, one launch (start us, length us, event | category | flops | bytes accessed | tf_op | source)
XLA Modules:
  0.0 56.5 jit_solution(12756124153865336365)
XLA Ops:
  0.6 0.0 copy-start
  0.6 1.0 %copy-done = bf16[32,56,128]{2,1,0:T(8,128)(2,1)S(1)} copy-done((bf16[32,56,128]{2,1,0:T(8,128)(2,1)S(1)}, bf16[32,56,128]{2,1,0:T(8,128)(2,1)}, u32[]{:S(2)}) %copy-start) | copy-done | bytes 458776
  1.7 0.0 copy-start.1
  1.7 1.0 %copy-done.1 = bf16[32,56,128]{2,1,0:T(8,128)(2,1)S(1)} copy-done((bf16[32,56,128]{2,1,0:T(8,128)(2,1)S(1)}, bf16[32,56,128]{2,1,0:T(8,128)(2,1)}, u32[]{:S(2)}) %copy-start.1) | copy-done | bytes 458776
  2.7 12.1 %halos.1 = (bf16[4,56,128]{2,1,0:T(8,128)(2,1)S(1)}, bf16[4,56,128]{2,1,0:T(8,128)(2,1)S(1)}, bf16[4,56,128]{2,1,0:T(8,128)(2,1)S(1)}, bf16[4,56,128]{2,1,0:T(8,...) custom-call(bf16[32,56,128]{2,1,0:T(8,128)(2,1)S(1)} %copy-done, ...), custom_call_target="tpu_custom_call" | custom-call | tf_op jit(solution)/shard_map/halos/pallas_call | solution.py:109
  14.8 0.0 copy-start.5
  14.8 0.6 %copy-done.5 = bf16[32,16,128]{2,1,0:T(8,128)(2,1)} copy-done((bf16[32,16,128]{2,1,0:T(8,128)(2,1)}, bf16[32,16,128]{2,1,0:T(8,128)(2,1)S(1)}, u32[]{:S(2)}) %copy-start.5) | copy-done | bytes 131096
  15.4 0.6 %copy-done.6 = bf16[32,16,128]{2,1,0:T(8,128)(2,1)} copy-done((bf16[32,16,128]{2,1,0:T(8,128)(2,1)}, bf16[32,16,128]{2,1,0:T(8,128)(2,1)S(1)}, u32[]{:S(2)}) %copy-start.6) | copy-done | bytes 131096
  16.1 0.6 %copy-done.7 = bf16[4,56,128]{2,1,0:T(8,128)(2,1)} copy-done((bf16[4,56,128]{2,1,0:T(8,128)(2,1)}, bf16[4,56,128]{2,1,0:T(8,128)(2,1)S(1)}, u32[]{:S(2)}) %copy-start.7) | copy-done | bytes 57368
  16.7 0.6 %copy-done.8 = bf16[4,56,128]{2,1,0:T(8,128)(2,1)} copy-done((bf16[4,56,128]{2,1,0:T(8,128)(2,1)}, bf16[4,56,128]{2,1,0:T(8,128)(2,1)S(1)}, u32[]{:S(2)}) %copy-start.8) | copy-done | bytes 57368
  17.3 0.6 %copy-done.9 = bf16[4,56,128]{2,1,0:T(8,128)(2,1)} copy-done((bf16[4,56,128]{2,1,0:T(8,128)(2,1)}, bf16[4,56,128]{2,1,0:T(8,128)(2,1)S(1)}, u32[]{:S(2)}) %copy-start.9) | copy-done | bytes 57368
  17.9 0.6 %copy-done.10 = bf16[4,56,128]{2,1,0:T(8,128)(2,1)} copy-done((bf16[4,56,128]{2,1,0:T(8,128)(2,1)}, bf16[4,56,128]{2,1,0:T(8,128)(2,1)S(1)}, u32[]{:S(2)}) %copy-start.10) | copy-done | bytes 57368
  18.5 0.6 %copy-done.11 = bf16[4,16,128]{2,1,0:T(8,128)(2,1)} copy-done((bf16[4,16,128]{2,1,0:T(8,128)(2,1)}, bf16[4,16,128]{2,1,0:T(8,128)(2,1)S(1)}, u32[]{:S(2)}) %copy-start.11) | copy-done | bytes 16408
  19.2 0.6 %copy-done.12 = bf16[4,16,128]{2,1,0:T(8,128)(2,1)} copy-done((bf16[4,16,128]{2,1,0:T(8,128)(2,1)}, bf16[4,16,128]{2,1,0:T(8,128)(2,1)S(1)}, u32[]{:S(2)}) %copy-start.12) | copy-done | bytes 16408
  19.8 0.6 %copy-done.13 = bf16[4,16,128]{2,1,0:T(8,128)(2,1)} copy-done((bf16[4,16,128]{2,1,0:T(8,128)(2,1)}, bf16[4,16,128]{2,1,0:T(8,128)(2,1)S(1)}, u32[]{:S(2)}) %copy-start.13) | copy-done | bytes 16408
  20.4 0.6 %copy-done.14 = bf16[4,16,128]{2,1,0:T(8,128)(2,1)} copy-done((bf16[4,16,128]{2,1,0:T(8,128)(2,1)}, bf16[4,16,128]{2,1,0:T(8,128)(2,1)S(1)}, u32[]{:S(2)}) %copy-start.14) | copy-done | bytes 16408
  21.0 11.7 %level.1 = (bf16[32,56,128]{2,1,0:T(8,128)(2,1)}, bf16[32,56,128]{2,1,0:T(8,128)(2,1)}, f32[1152,128]{1,0:T(8,128)}, f32[1152,256]{1,0:T(8,128)}, f32[1024,128]{1,0:T(8,128)}) custom-call(bf16[32,56,128]{2,1,0:T(8,128)(2,1)} %refs_0_.1, bf16[32,56,128]{2,1,0:T(8,128)(2,1)} %refs_1_.1, bf16[4,56,128]{2,1,0:T(8,128)(2,1)} %copy-done.7, ...), custom_call_target="tpu_custom_call" | custom-call | tf_op jit(solution)/shard_map/level/pallas_call | solution.py:339
  32.7 1.3 %copy-done.2 = f32[1152,256]{1,0:T(8,128)S(1)} copy-done((f32[1152,256]{1,0:T(8,128)S(1)}, f32[1152,256]{1,0:T(8,128)}, u32[]{:S(2)}) %copy-start.2) | copy-done | bytes 1179672
  34.0 1.1 %copy-done.3 = f32[1152,128]{1,0:T(8,128)S(1)} copy-done((f32[1152,128]{1,0:T(8,128)S(1)}, f32[1152,128]{1,0:T(8,128)}, u32[]{:S(2)}) %copy-start.3) | copy-done | bytes 589848
  35.0 1.0 %copy-done.4 = f32[1024,128]{1,0:T(8,128)S(1)} copy-done((f32[1024,128]{1,0:T(8,128)S(1)}, f32[1024,128]{1,0:T(8,128)}, u32[]{:S(2)}) %copy-start.4) | copy-done | bytes 524312
  36.1 18.5 %sums.1 = (f32[36,128]{1,0:T(8,128)S(1)}, f32[36,256]{1,0:T(8,128)S(1)}, f32[32,128]{1,0:T(8,128)S(1)}) custom-call(f32[1152,128]{1,0:T(8,128)S(1)} %copy-done.3, f32[1152,256]{1,0:T(8,128)S(1)} %copy-done.2, f32[1024,128]{1,0:T(8,128)S(1)} %copy-done.4), custom_call_target="tpu_custom_call" | custom-call | tf_op jit(solution)/shard_map/sums/pallas_call | solution.py:446
  54.6 0.6 %reshape.20 = f32[9216]{0:T(1024)} reshape(f32[36,256]{1,0:T(8,128)S(1)} %get-tuple-element.39) | data formatting | bytes 73728 | tf_op jit(solution)/shard_map/reshape | solution.py:481
  55.3 0.6 %copy.12 = f32[4608]{0:T(1024)} copy(f32[4608]{0:T(1024)S(1)} %bitcast.2) | data formatting | bytes 36864
  55.9 0.6 %copy.13 = f32[4096]{0:T(1024)} copy(f32[4096]{0:T(1024)S(1)} %bitcast.3) | data formatting | bytes 32768
  (12 shorter events, 0.0 us)
Async XLA Ops:
  0.6 1.0 %copy-start = (bf16[32,56,128]{2,1,0:T(8,128)(2,1)S(1)}, bf16[32,56,128]{2,1,0:T(8,128)(2,1)}, u32[]{:S(2)}) copy-start(bf16[32,56,128]{2,1,0:T(8,128)(2,1)} %refs_0_.1) | copy-start | bytes 1376260
  1.7 1.0 %copy-start.1 = (bf16[32,56,128]{2,1,0:T(8,128)(2,1)S(1)}, bf16[32,56,128]{2,1,0:T(8,128)(2,1)}, u32[]{:S(2)}) copy-start(bf16[32,56,128]{2,1,0:T(8,128)(2,1)} %refs_1_.1) | copy-start | bytes 1376260
  14.8 0.6 %copy-start.5 = (bf16[32,16,128]{2,1,0:T(8,128)(2,1)}, bf16[32,16,128]{2,1,0:T(8,128)(2,1)S(1)}, u32[]{:S(2)}) copy-start(bf16[32,16,128]{2,1,0:T(8,128)(2,1)S(1)} %get-tuple-element.27.refs_6_) | copy-start | bytes 393220
  15.4 0.6 %copy-start.6 = (bf16[32,16,128]{2,1,0:T(8,128)(2,1)}, bf16[32,16,128]{2,1,0:T(8,128)(2,1)S(1)}, u32[]{:S(2)}) copy-start(bf16[32,16,128]{2,1,0:T(8,128)(2,1)S(1)} %get-tuple-element.28.refs_7_) | copy-start | bytes 393220
  16.1 0.6 %copy-start.7 = (bf16[4,56,128]{2,1,0:T(8,128)(2,1)}, bf16[4,56,128]{2,1,0:T(8,128)(2,1)S(1)}, u32[]{:S(2)}) copy-start(bf16[4,56,128]{2,1,0:T(8,128)(2,1)S(1)} %get-tuple-element.23.refs_2_) | copy-start | bytes 172036
  16.7 0.6 %copy-start.8 = (bf16[4,56,128]{2,1,0:T(8,128)(2,1)}, bf16[4,56,128]{2,1,0:T(8,128)(2,1)S(1)}, u32[]{:S(2)}) copy-start(bf16[4,56,128]{2,1,0:T(8,128)(2,1)S(1)} %get-tuple-element.24.refs_3_) | copy-start | bytes 172036
  17.3 0.6 %copy-start.9 = (bf16[4,56,128]{2,1,0:T(8,128)(2,1)}, bf16[4,56,128]{2,1,0:T(8,128)(2,1)S(1)}, u32[]{:S(2)}) copy-start(bf16[4,56,128]{2,1,0:T(8,128)(2,1)S(1)} %get-tuple-element.25.refs_4_) | copy-start | bytes 172036
  17.9 0.6 %copy-start.10 = (bf16[4,56,128]{2,1,0:T(8,128)(2,1)}, bf16[4,56,128]{2,1,0:T(8,128)(2,1)S(1)}, u32[]{:S(2)}) copy-start(bf16[4,56,128]{2,1,0:T(8,128)(2,1)S(1)} %get-tuple-element.26.refs_5_) | copy-start | bytes 172036
  18.5 0.6 %copy-start.11 = (bf16[4,16,128]{2,1,0:T(8,128)(2,1)}, bf16[4,16,128]{2,1,0:T(8,128)(2,1)S(1)}, u32[]{:S(2)}) copy-start(bf16[4,16,128]{2,1,0:T(8,128)(2,1)S(1)} %get-tuple-element.29.refs_8_) | copy-start | bytes 49156
  19.2 0.6 %copy-start.12 = (bf16[4,16,128]{2,1,0:T(8,128)(2,1)}, bf16[4,16,128]{2,1,0:T(8,128)(2,1)S(1)}, u32[]{:S(2)}) copy-start(bf16[4,16,128]{2,1,0:T(8,128)(2,1)S(1)} %get-tuple-element.30.refs_9_) | copy-start | bytes 49156
  19.8 0.6 %copy-start.13 = (bf16[4,16,128]{2,1,0:T(8,128)(2,1)}, bf16[4,16,128]{2,1,0:T(8,128)(2,1)S(1)}, u32[]{:S(2)}) copy-start(bf16[4,16,128]{2,1,0:T(8,128)(2,1)S(1)} %get-tuple-element.31.refs_10_) | copy-start | bytes 49156
  20.4 0.6 %copy-start.14 = (bf16[4,16,128]{2,1,0:T(8,128)(2,1)}, bf16[4,16,128]{2,1,0:T(8,128)(2,1)S(1)}, u32[]{:S(2)}) copy-start(bf16[4,16,128]{2,1,0:T(8,128)(2,1)S(1)} %get-tuple-element.32.refs_11_) | copy-start | bytes 49156
  32.7 1.3 %copy-start.2 = (f32[1152,256]{1,0:T(8,128)S(1)}, f32[1152,256]{1,0:T(8,128)}, u32[]{:S(2)}) copy-start(f32[1152,256]{1,0:T(8,128)} %get-tuple-element.36.down) | copy-start | bytes 3538948
  34.0 1.1 %copy-start.3 = (f32[1152,128]{1,0:T(8,128)S(1)}, f32[1152,128]{1,0:T(8,128)}, u32[]{:S(2)}) copy-start(f32[1152,128]{1,0:T(8,128)} %get-tuple-element.35.conv) | copy-start | bytes 1769476
  35.0 1.0 %copy-start.4 = (f32[1024,128]{1,0:T(8,128)S(1)}, f32[1024,128]{1,0:T(8,128)}, u32[]{:S(2)}) copy-start(f32[1024,128]{1,0:T(8,128)} %get-tuple-element.37.up) | copy-start | bytes 1572868

commit v2 on v1

v2 whole, which is shorter than its diff:
```python
import functools
import math

import jax
import jax.numpy as jnp
from jax import lax
from jax.experimental import pallas as pl
from jax.experimental.pallas import tpu as pltpu
from jax.sharding import PartitionSpec as P

MESH = pl.DeviceIdType.MESH
F32 = jnp.float32
BF16 = jnp.bfloat16
VMEM = pl.BlockSpec(memory_space=pltpu.VMEM)
NT = (((1,), (1,)), ((), ()))
TN = (((0,), (0,)), ((), ()))
SHIFTS = [(dr, dc) for dr in (-1, 0, 1) for dc in (-1, 0, 1) if (dr, dc) != (0, 0)]


def dot(a, b):
    return jnp.dot(a, b, preferred_element_type=F32)


def dot_nt(a, b):
    return lax.dot_general(a, b, NT, preferred_element_type=F32)


def dot_tn(a, b):
    return lax.dot_general(a, b, TN, preferred_element_type=F32)


def exists(at, n, d):
    return at > 0 if d < 0 else at < n - 1


def level_kernel(n_row, n_col, reduce, *refs):
    x_hbm, ct_hbm, wc_hbm, wd_hbm, wu_hbm, out_hbm, gx_hbm, conv_out, down_out, up_out = refs[:10]
    x_ref, ct_ref, wc, wd, wu, out_ref, gx_ref, pack = refs[10:18]
    x_top, x_bot, ct_top, ct_bot, left, right, tl, tr, bl, br = edges = refs[18:28]
    (xf, x3, ce, fine, slope, d3, t4, cp, co, g, gp, g3, up) = refs[28:41]
    send_sem, recv_sem, local_sem = refs[41:44]
    conv_sum, down_sum, up_sum = refs[44:47] if reduce else (conv_out, down_out, up_out)
    rows, cols, ch = x_ref.shape
    wide = wd.shape[3]
    nz = n_col // 2
    r, c = lax.axis_index("row"), lax.axis_index("col")
    z, core = c // 2, c % 2
    has_top, has_bot = r > 0, r < n_row - 1
    has_left, has_right = c > 0, c < n_col - 1
    ce_rows, a_rows, u_rows = rows + 4, rows + 6, rows // 2 + 2
    half = rows // 2

    loads = [
        pltpu.make_async_copy(src, dst, local_sem.at[k])
        for k, (src, dst) in enumerate(
            [(x_hbm, x_ref), (ct_hbm, ct_ref), (wc_hbm, wc), (wd_hbm, wd), (wu_hbm, wu)]
        )
    ]
    for item in loads:
        item.start()

    def near(dr, dc):
        ok = None
        for d, at, n in ((dr, r, n_row), (dc, c, n_col)):
            if d:
                here = exists(at, n, d)
                ok = here if ok is None else jnp.logical_and(ok, here)
        return ok

    peers = [(r, z * 2 + 1 - core)]
    peers += [((r + k) % n_row, c) for k in range(1, n_row)]
    peers += [(r, ((z + k) % nz) * 2 + core) for k in range(1, nz)]
    if not reduce:
        peers = []
    barrier = pltpu.get_barrier_semaphore()
    for dr, dc in SHIFTS:

        @pl.when(near(dr, dc))
        def _(dr=dr, dc=dc):
            pl.semaphore_signal(barrier, inc=1, device_id=(r + dr, c + dc), device_id_type=MESH)

    for peer in peers:
        pl.semaphore_signal(barrier, inc=1, device_id=peer, device_id_type=MESH)

    loads[0].wait()
    loads[1].wait()
    for side, at in ((0, 0), (1, cols - 8)):
        pack[side] = jnp.concatenate(
            [x_ref[:, at : at + 8, :].astype(F32), ct_ref[:, at : at + 8, :].astype(F32)], axis=1
        ).astype(BF16)
    near_r = 3 - (r == 0).astype(jnp.int32) - (r == n_row - 1).astype(jnp.int32)
    near_c = 3 - (c == 0).astype(jnp.int32) - (c == n_col - 1).astype(jnp.int32)
    pl.semaphore_wait(barrier, near_r * near_c - 1 + len(peers))

    low, high = pl.ds(0, 4), pl.ds(rows - 4, 4)
    plan = [
        ((1, 0), x_ref.at[high], x_top),
        ((-1, 0), x_ref.at[low], x_bot),
        ((1, 0), ct_ref.at[pl.ds(rows - 2, 2)], ct_top),
        ((-1, 0), ct_ref.at[pl.ds(0, 2)], ct_bot),
        ((0, 1), pack.at[1], left),
        ((0, -1), pack.at[0], right),
        ((1, 1), pack.at[1, high], tl),
        ((1, -1), pack.at[0, high], tr),
        ((-1, 1), pack.at[1, low], bl),
        ((-1, -1), pack.at[0, low], br),
    ]

    def remote(k, src, dst, device):
        return pltpu.make_async_remote_copy(
            src_ref=src,
            dst_ref=dst,
            send_sem=send_sem.at[k],
            recv_sem=recv_sem.at[k],
            device_id=device,
            device_id_type=MESH,
        )

    def edge(k):
        (dr, dc), src, dst = plan[k]
        return remote(k, src, dst, (r + dr, c + dc))

    for k, ((dr, dc), _, _) in enumerate(plan):

        @pl.when(near(dr, dc))
        def _(k=k):
            edge(k).start()

    xf[:, 64:72, :] = jnp.zeros((rows + 8, 8, ch), F32)
    ce[:, 64:72, :] = jnp.zeros((ce_rows, 8, ch), F32)
    fine[:, 64:72, :] = jnp.zeros((a_rows, 8, ch), F32)
    slope[:, 64:72, :] = jnp.zeros((a_rows, 8, ch), F32)
    gp[:, 64:72, :] = jnp.zeros((a_rows, 8, ch), F32)

    @pl.loop(0, rows // 4)
    def _(k):
        at = pl.ds(k * 4, 4)
        xf[pl.ds(4 + k * 4, 4), 4 : 4 + cols, :] = x_ref[at].astype(F32)
        ce[pl.ds(2 + k * 4, 4), 3 : 3 + cols, :] = ct_ref[at].astype(F32)

    for item in loads[2:]:
        item.wait()
    for k, ((dr, dc), _, _) in enumerate(plan):

        @pl.when(near(dr, dc))
        def _(k=k):
            edge(k).wait_send()

        @pl.when(near(-dr, -dc))
        def _(k=k):
            edge(k).wait_recv()

    def sides(dst, offset, at, lft, rgt, row_ok):
        ok_l, ok_r = has_left, has_right
        if row_ok is not None:
            ok_l = jnp.logical_and(ok_l, row_ok)
            ok_r = jnp.logical_and(ok_r, row_ok)
        rows_at = pl.ds(at, lft.shape[0])
        dst[rows_at, 0:offset, :] = jnp.where(ok_l, lft.astype(F32), 0.0)[:, 8 - offset : 8, :]
        dst[rows_at, offset + cols : offset + cols + 8, :] = jnp.where(ok_r, rgt.astype(F32), 0.0)

    xs, cs = slice(0, 8), slice(8, 16)
    for dst, offset, at, own, row_ok in (
        (xf, 4, 0, x_top, has_top),
        (xf, 4, rows + 4, x_bot, has_bot),
        (ce, 3, 0, ct_top, has_top),
        (ce, 3, rows + 2, ct_bot, has_bot),
    ):
        dst[at : at + own.shape[0], offset : offset + cols, :] = jnp.where(
            row_ok, own[...].astype(F32), 0.0
        )
    sides(xf, 4, 0, tl[:, xs, :], tr[:, xs, :], has_top)
    sides(xf, 4, rows + 4, bl[:, xs, :], br[:, xs, :], has_bot)
    sides(ce, 3, 0, tl[2:4, cs, :], tr[2:4, cs, :], has_top)
    sides(ce, 3, rows + 2, bl[0:2, cs, :], br[0:2, cs, :], has_bot)

    @pl.loop(0, rows // 8)
    def _(k):
        at = pl.ds(k * 8, 8)
        sides(xf, 4, 4 + k * 8, left[at, xs, :], right[at, xs, :], None)
        sides(ce, 3, 2 + k * 8, left[at, cs, :], right[at, cs, :], None)

    per_core = n_row * nz
    n_peers = n_row + nz - 1

    def stage_all(part, pieces_of):
        stage = parts[part][0]
        for row in range(n_row):
            for col in range(n_col):
                pieces = pieces_of(row * n_col + col)
                pad = stage.shape[1] - sum(p.shape[0] for p in pieces)
                if pad:
                    pieces.append(jnp.zeros((pad, 128), F32))
                slot = (col % 2) * per_core + row * nz + col // 2
                stage[slot] = jnp.concatenate(pieces, axis=0).astype(BF16)

    def sum_copies(part, level):
        stage, recv0, acc1, recv1, acc2, recv2 = parts[part]
        if level == 0:
            todo = [(0, stage.at[pl.ds((1 - core) * per_core, per_core)], recv0)]
        elif level == 1:
            todo = [(k, acc1.at[(r + k) % n_row], recv1.at[k - 1]) for k in range(1, n_row)]
        else:
            todo = [
                (n_row - 1 + k, acc2.at[(z + k) % nz], recv2.at[k - 1]) for k in range(1, nz)
            ]
        base = 10 + part * n_peers
        return [remote(base + k, src, dst, peers[k]) for k, src, dst in todo]

    def start_sums(part, level):
        if reduce:
            for item in sum_copies(part, level):
                item.start()

    def finish_sums(part, level):
        if not reduce:
            return None
        for item in sum_copies(part, level):
            item.wait()
        stage, recv0, acc1, recv1, acc2, recv2 = parts[part]
        if level == 0:
            for k in range(per_core):
                own = stage[core * per_core + k].astype(F32)
                acc1[k // nz, k % nz] = (own + recv0[k].astype(F32)).astype(BF16)
        elif level == 1:
            for k in range(nz):
                total = acc1[r, k].astype(F32)
                for m in range(n_row - 1):
                    total = total + recv1[m, k].astype(F32)
                acc2[k] = total.astype(BF16)
        else:
            total = acc2[z].astype(F32)
            for m in range(nz - 1):
                total = total + recv2[m].astype(F32)
            return total * scale
        return None

    parts = (refs[47:53], refs[53:59])
    scale = 1.0 / math.sqrt(rows * n_row * cols * n_col)
    blocks = n_row * n_col
    nc, nd, nu = 9 * ch // blocks, 9 * ch // blocks, 4 * wide // blocks

    @pl.loop(0, (rows + 8) // 4)
    def _(k):
        at = pl.ds(k * 4, 4)
        for q in range(3):
            x3[at, :, q * ch : (q + 1) * ch] = xf[at, q : q + 64, :].astype(BF16)

    wc_rows = wc[...].reshape(3, 3 * ch, ch)
    j_at = lax.broadcasted_iota(jnp.int32, (1, 64, 1), 1) - 3
    col_ok = jnp.logical_and(
        jnp.logical_or(j_at >= 0, has_left), jnp.logical_or(j_at < cols, has_right)
    )
    def in_grid(first, n):
        i_at = lax.broadcasted_iota(jnp.int32, (n, 1, 1), 0) + (first - 3)
        row_ok = jnp.logical_and(
            jnp.logical_or(i_at >= 0, has_top), jnp.logical_or(i_at < rows, has_bot)
        )
        return jnp.logical_and(row_ok, col_ok)

    step = a_rows // 2

    @pl.loop(0, 2)
    def _(k):
        pre = None
        for p in range(3):
            term = dot(x3[pl.ds(k * step + p, step)].reshape(step * 64, 3 * ch), wc_rows[p])
            pre = term if pre is None else pre + term
        sig = jax.nn.sigmoid(pre)
        at = pl.ds(k * step, step)
        ok = in_grid(k * step, step)
        value = (pre * sig).reshape(step, 64, ch)
        fine[at, 0:64, :] = jnp.where(ok, value, 0.0)
        slope[at, 0:64, :] = (sig * (1.0 + pre * (1.0 - sig))).reshape(step, 64, ch)

    @pl.loop(0, a_rows // 2)
    def _(k):
        for p in range(2):
            for q in range(3):
                d3[k, p, :, q * ch : (q + 1) * ch] = fine[
                    2 * k + p, pl.ds(q, 32, stride=2), :
                ].astype(BF16)

    @pl.loop(0, u_rows)
    def _(k):
        for p in range(2):
            for q in range(2):
                e = 2 * p + q
                t4[k, :, e * ch : (e + 1) * ch] = ce[
                    2 * k + p, pl.ds(1 + q, 32, stride=2), :
                ].astype(BF16)

    wd_rows = wd[...].reshape(3, 3 * ch, wide)
    cpre = None
    for p in range(3):
        window = d3[p // 2 : p // 2 + u_rows, p % 2].reshape(u_rows * 32, 3 * ch)
        term = dot(window, wd_rows[p])
        cpre = term if cpre is None else cpre + term
    cp[...] = cpre.reshape(u_rows, 32, wide)
    v_at = lax.broadcasted_iota(jnp.int32, (1, 32, 1), 1) - 1
    v_own = jnp.logical_and(v_at >= 0, v_at < cols // 2)
    sig = jax.nn.sigmoid(cp[...])
    co[...] = (cp[...] * sig).astype(BF16)
    grad = None
    for e in range(4):
        term = dot_nt(
            t4[:, :, e * ch : (e + 1) * ch].reshape(u_rows * 32, ch), wu[e // 2, e % 2]
        )
        grad = term if grad is None else grad + term
    u_at = lax.broadcasted_iota(jnp.int32, (u_rows, 1, 1), 0) - 1
    ok = jnp.logical_and(
        jnp.logical_and(jnp.logical_or(u_at >= 0, has_top), jnp.logical_or(u_at < half, has_bot)),
        jnp.logical_and(
            jnp.logical_or(v_at >= 0, has_left), jnp.logical_or(v_at < cols // 2, has_right)
        ),
    )
    full = cp[...]
    sig = jax.nn.sigmoid(full)
    part = grad.reshape(u_rows, 32, wide) * (sig * (1.0 + full * (1.0 - sig)))
    g[:, 32:40, :] = jnp.zeros((u_rows, 8, wide), F32)
    g[:, 0:32, :] = jnp.where(ok, part, 0.0)

    own_co = jnp.where(v_own, co[1 : half + 1].astype(F32), 0.0).astype(BF16)
    us = dot_tn(own_co.reshape(half * 32, wide), t4[1 : half + 1].reshape(half * 32, 4 * ch))
    for e in range(4):
        up_sum[e * wide : (e + 1) * wide, :] = us[:, e * ch : (e + 1) * ch]
    own_g = jnp.where(v_own, g[1 : half + 1, 0:32, :], 0.0).astype(BF16).reshape(half * 32, wide)
    for p in range(3):
        window = d3[p // 2 + 1 : p // 2 + 1 + half, p % 2].reshape(half * 32, 3 * ch)
        down_sum[p * 3 * ch : (p + 1) * 3 * ch, :] = dot_tn(window, own_g)

    if reduce:
        stage_all(
            0,
            lambda d: [
                up_sum[d * nu : (d + 1) * nu, :],
                down_sum[d * nd : (d + 1) * nd, 0:128],
                down_sum[d * nd : (d + 1) * nd, 128:256],
            ],
        )
    start_sums(0, 0)

    co_rows = co[1 : half + 1].reshape(half * 32, wide)
    for e in range(4):
        p, q = e // 2, e % 2
        res = dot(co_rows, wu[p, q]).reshape(half, 32, ch)
        for m in range(half):
            up[2 * m + p, pl.ds(1 + q, 32, stride=2), :] = res[m]

    @pl.loop(0, rows // 4)
    def _(k):
        f = fine[pl.ds(3 + k * 4, 4), 3 : 3 + cols, :].astype(BF16).astype(F32)
        out_ref[pl.ds(k * 4, 4)] = (f + up[pl.ds(k * 4, 4), 3 : 3 + cols, :]).astype(BF16)

    out_copy = pltpu.make_async_copy(out_ref, out_hbm, local_sem.at[5])
    out_copy.start()
    finish_sums(0, 0)
    start_sums(0, 1)

    g_here = g[:, 0:32, :].astype(BF16).reshape(u_rows * 32, wide)
    g_next = g[:, 1:33, :].astype(BF16).reshape(u_rows * 32, wide)
    less = (u_rows - 1) * 32

    def pair(p):
        return jnp.concatenate([wd[p, 1], wd[p, 2]], axis=0)

    even = dot_nt(g_here, pair(1))
    even_odd = even[:, ch:] + dot_nt(g_next, wd[1, 0])
    odd = dot_nt(g_here[32:], pair(0)) + dot_nt(g_here[:less], pair(2))
    odd_odd = odd[:, ch:] + dot_nt(g_next[32:], wd[0, 0]) + dot_nt(g_next[:less], wd[2, 0])
    spread = {
        (0, 0): even[:, :ch],
        (0, 1): even_odd,
        (1, 0): odd[:, :ch],
        (1, 1): odd_odd,
    }
    for (s, t), value in spread.items():
        for u in range(u_rows - s):
            at = pl.ds(1 + t, 32, stride=2)
            ce[2 * u + s, at, :] = ce[2 * u + s, at, :] + value[u * 32 : (u + 1) * 32]

    @pl.loop(0, (rows + 2) // 2)
    def _(k):
        a = 2 + 2 * k
        value = ce[pl.ds(a - 1, 2), 0:64, :] * slope[pl.ds(a, 2), 0:64, :]
        gp[pl.ds(a, 2), 0:64, :] = jnp.where(in_grid(a, 2), value, 0.0)

    @pl.loop(0, (rows + 2) // 2)
    def _(k):
        at = pl.ds(2 + 2 * k, 2)
        for q in range(3):
            g3[at, :, q * ch : (q + 1) * ch] = gp[at, 4 - q : 68 - q, :].astype(BF16)

    j_own = jnp.logical_and(j_at >= 0, j_at < cols)
    own = jnp.where(j_own, gp[3 : rows + 3, 0:64, :], 0.0).astype(BF16)

    def shift(p):
        pieces = [own]
        if p > 0:
            pieces.insert(0, jnp.zeros((p, 64, ch), BF16))
        if p < 2:
            pieces.append(jnp.zeros((2 - p, 64, ch), BF16))
        return jnp.concatenate(pieces, axis=0).reshape((rows + 2) * 64, ch)

    shifted = [shift(p) for p in range(3)]
    sums = dot_tn(
        x3[3 : rows + 5].reshape((rows + 2) * 64, 3 * ch), jnp.concatenate(shifted, axis=1)
    )
    for p in range(3):
        conv_sum[p * 3 * ch : (p + 1) * 3 * ch, :] = sums[:, p * ch : (p + 1) * ch]

    if reduce:
        stage_all(1, lambda d: [conv_sum[d * nc : (d + 1) * nc, :]])
    start_sums(1, 0)
    finish_sums(0, 1)
    start_sums(0, 2)

    turned = [jnp.concatenate([wc[p, q] for q in range(3)], axis=1) for p in range(3)]
    part_rows = rows // 2

    def half_inputs(k):
        total = None
        for p in range(3):
            first = k * part_rows + 4 - p
            window = g3[first : first + part_rows].reshape(part_rows * 64, 3 * ch)
            term = dot_nt(window, turned[p])
            total = term if total is None else total + term
        total = total.reshape(part_rows, 64, ch)[:, :cols, :]
        at = pl.ds(k * part_rows, part_rows)
        gx_ref[at] = total.astype(BF16)
        done = pltpu.make_async_copy(gx_ref.at[at], gx_hbm.at[at], local_sem.at[6 + k])
        done.start()
        return done

    first_half = half_inputs(0)
    finish_sums(1, 0)
    start_sums(1, 1)
    second_half = half_inputs(1)
    finish_sums(1, 1)
    start_sums(1, 2)
    total = finish_sums(0, 2)
    if reduce:
        up_out[...] = total[0:nu]
        down_out[:, 0:128] = total[nu : nu + nd]
        down_out[:, 128:256] = total[nu + nd : nu + 2 * nd]
    total = finish_sums(1, 2)
    if reduce:
        conv_out[...] = total[0:nc]
    for item in (out_copy, first_half, second_half):
        item.wait()


def body(n_row, n_col, x, ct, wc, wd, wu):
    rows, cols, ch = x.shape
    wide = wd.shape[3]
    a_rows, u_rows = rows + 6, rows // 2 + 2
    blocks, nz = n_row * n_col, n_col // 2
    sums = [(9 * ch, ch), (9 * ch, wide), (4 * wide, ch)]
    reduce = all(n % blocks == 0 for n, _ in sums)
    edges = [(4, cols, ch)] * 2 + [(2, cols, ch)] * 2 + [(rows, 16, ch)] * 2 + [(4, 16, ch)] * 4
    n_sems = 10
    scratch = [pltpu.VMEM(a.shape, BF16) for a in (x, ct, wc, wd, wu, x, x)]
    scratch += [pltpu.VMEM((2, rows, 16, ch), BF16)]
    scratch += [pltpu.VMEM(e, BF16) for e in edges]
    scratch += [
        pltpu.VMEM((rows + 8, 72, ch), F32),
        pltpu.VMEM((rows + 8, 64, 3 * ch), BF16),
        pltpu.VMEM((rows + 4, 72, ch), F32),
        pltpu.VMEM((a_rows, 72, ch), F32),
        pltpu.VMEM((a_rows, 72, ch), F32),
        pltpu.VMEM((a_rows // 2, 2, 32, 3 * ch), BF16),
        pltpu.VMEM((u_rows, 32, 4 * ch), BF16),
        pltpu.VMEM((u_rows, 32, wide), F32),
        pltpu.VMEM((u_rows, 32, wide), BF16),
        pltpu.VMEM((u_rows, 40, wide), F32),
        pltpu.VMEM((a_rows, 72, ch), F32),
        pltpu.VMEM((a_rows, 64, 3 * ch), BF16),
        pltpu.VMEM((rows, 72, ch), F32),
    ]
    more = []
    if reduce:
        n_sems += 2 * (n_row + nz - 1)
        more += [pltpu.VMEM(s, F32) for s in sums]
        heights = (sums[2][0] + 2 * sums[1][0]) // blocks, sums[0][0] // blocks
        for height in heights:
            height = -(-height // 16) * 16
            for lead in (
                (blocks,), (blocks // 2,), (n_row, nz), (n_row - 1, nz), (nz,), (nz - 1,)
            ):
                more.append(pltpu.VMEM(lead + (height, 128), BF16))
        outs = [(n // blocks, w) for n, w in sums]
    else:
        outs = sums
    scratch += [pltpu.SemaphoreType.DMA((n_sems,))] * 2 + [pltpu.SemaphoreType.DMA((8,))] + more
    anywhere = pl.BlockSpec(memory_space=pl.ANY)
    output, grad_inputs, *sums = pl.pallas_call(
        functools.partial(level_kernel, n_row, n_col, reduce),
        out_shape=[jax.ShapeDtypeStruct(x.shape, BF16)] * 2
        + [jax.ShapeDtypeStruct(s, F32) for s in outs],
        in_specs=[anywhere] * 5,
        out_specs=[anywhere] * 2 + [VMEM] * 3,
        scratch_shapes=scratch,
        compiler_params=pltpu.CompilerParams(
            collective_id=0, has_side_effects=True, vmem_limit_bytes=60 * 2**20
        ),
        name="level",
    )(x, ct, wc, wd, wu)
    sums = [a.reshape(-1) for a in sums]
    if not reduce:
        scale = 1.0 / math.sqrt(rows * n_row * cols * n_col)
        sums = [
            lax.psum_scatter(a, ("row", "col"), scatter_dimension=0, tiled=True) * scale
            for a in sums
        ]
    return (output, grad_inputs, *sums)


def solution(mesh):
    return jax.shard_map(
        functools.partial(body, mesh.shape["row"], mesh.shape["col"]),
        mesh=mesh,
        in_specs=(P("row", "col", None), P("row", "col", None), P(), P(), P()),
        out_specs=(
            P("row", "col", None),
            P("row", "col", None),
            P(("row", "col")),
            P(("row", "col")),
            P(("row", "col")),
        ),
        check_vma=False,
    )
```

time: 56.8 us -> 41.9 us (0.74)
  local copies, waits for them, and re-layouts: 13.4 us -> 5.38 us
  Pallas kernels: 42.4 us -> 35.6 us
    unnamed x32 -> x10, local copies, waits for them, and re-layouts: 12.8 us -> 3.98 us
    pallas_call x3 -> x1, Pallas kernels: 42.4 us -> 35.6 us  [body(): pl.pallas_call(functools.partial(level_kernel, n_row, n_col, reduce), out...]
    reshape x1, local copies, waits for them, and re-layouts: 0.62 us -> 1.4 us  [body(): sums = [a.reshape(-1) for a in sums]]
where the time goes in v2:
time: 41.9 us; the launch traced here: 41.6 us
  Pallas kernels  35.6 us (85%)
  local copies, waits for them, and re-layouts  5.38 us (13%)
  between operations  0.65 us (2%)
    pallas_call x1, Pallas kernels, body(): pl.pallas_call(functools.partial(level_kernel, n_row, n_col, reduce), out...  35.6 us
    unnamed x10, local copies, waits for them, and re-layouts  3.98 us
    reshape x1, local copies, waits for them, and re-layouts, body(): sums = [a.reshape(-1) for a in sums]  1.4 us

profile of v2, /device:TPU:0, one launch (start us, length us, event | category | flops | bytes accessed | tf_op | source)
XLA Modules:
  0.0 41.6 jit_solution(17513298537060887719)
XLA Ops:
  0.6 35.6 %level.1 = (bf16[32,56,128]{2,1,0:T(8,128)(2,1)}, bf16[32,56,128]{2,1,0:T(8,128)(2,1)}, f32[36,128]{1,0:T(8,128)}, f32[36,256]{1,0:T(8,128)}, f32[32,128]{1,0:T(8,128)}) custom-call(bf16[32,56,128]{2,1,0:T(8,128)(2,1)} %refs_0_.1, bf16[32,56,128]{2,1,0:T(8,128)(2,1)} %refs_1_.1, bf16[3,3,128,128]{3,2,1,0:T(8,128)(2,1)} %refs_2_.1, ...), custom_call_target="tpu_custom_call" | custom-call | tf_op jit(solution)/shard_map/level/pallas_call | solution.py:496
  36.2 1.4 %reshape.20 = f32[9216]{0:T(1024)} reshape(f32[36,256]{1,0:T(8,128)} %get-tuple-element.13) | data formatting | bytes 73728 | tf_op jit(solution)/shard_map/reshape | solution.py:508
  37.6 0.0 copy-start
  37.6 1.9 %copy.14 = bf16[32,56,128]{2,1,0:T(8,128)(2,1)} copy(bf16[32,56,128]{2,1,0:T(8,128)(2,1)} %get-tuple-element.20) | data formatting | bytes 917504
  39.5 0.0 copy-done
  39.5 0.0 copy-start.1
  39.5 0.8 %copy.15 = bf16[32,56,128]{2,1,0:T(8,128)(2,1)} copy(bf16[32,56,128]{2,1,0:T(8,128)(2,1)S(1)} %copy-done) | data formatting | bytes 917504
  40.3 0.0 copy-done.1
  40.3 0.0 copy-start.2
  40.3 0.6 %copy.16 = f32[4608]{0:T(1024)} copy(f32[4608]{0:T(1024)S(1)} %bitcast.2) | data formatting | bytes 36864
  40.9 0.1 copy-done.2
  41.0 0.6 %copy.17 = f32[4096]{0:T(1024)} copy(f32[4096]{0:T(1024)S(1)} %bitcast.3) | data formatting | bytes 32768
Async XLA Ops:
  37.6 1.9 %copy-start = (bf16[32,56,128]{2,1,0:T(8,128)(2,1)S(1)}, bf16[32,56,128]{2,1,0:T(8,128)(2,1)}, u32[]{:S(2)}) copy-start(bf16[32,56,128]{2,1,0:T(8,128)(2,1)} %get-tuple-element.21) | copy-start | bytes 1376260
  39.5 0.8 %copy-start.1 = (f32[36,128]{1,0:T(8,128)S(1)}, f32[36,128]{1,0:T(8,128)}, u32[]{:S(2)}) copy-start(f32[36,128]{1,0:T(8,128)} %get-tuple-element.12) | copy-start | bytes 55300
  40.3 0.7 %copy-start.2 = (f32[32,128]{1,0:T(8,128)S(1)}, f32[32,128]{1,0:T(8,128)}, u32[]{:S(2)}) copy-start(f32[32,128]{1,0:T(8,128)} %get-tuple-element.14) | copy-start | bytes 49156

commit v3 on v2

--- a/solution.py
+++ b/solution.py
@@ -340,23 +340,6 @@
         )
     start_sums(0, 0)
 
-    co_rows = co[1 : half + 1].reshape(half * 32, wide)
-    for e in range(4):
-        p, q = e // 2, e % 2
-        res = dot(co_rows, wu[p, q]).reshape(half, 32, ch)
-        for m in range(half):
-            up[2 * m + p, pl.ds(1 + q, 32, stride=2), :] = res[m]
-
-    @pl.loop(0, rows // 4)
-    def _(k):
-        f = fine[pl.ds(3 + k * 4, 4), 3 : 3 + cols, :].astype(BF16).astype(F32)
-        out_ref[pl.ds(k * 4, 4)] = (f + up[pl.ds(k * 4, 4), 3 : 3 + cols, :]).astype(BF16)
-
-    out_copy = pltpu.make_async_copy(out_ref, out_hbm, local_sem.at[5])
-    out_copy.start()
-    finish_sums(0, 0)
-    start_sums(0, 1)
-
     g_here = g[:, 0:32, :].astype(BF16).reshape(u_rows * 32, wide)
     g_next = g[:, 1:33, :].astype(BF16).reshape(u_rows * 32, wide)
     less = (u_rows - 1) * 32
@@ -379,6 +362,9 @@
             at = pl.ds(1 + t, 32, stride=2)
             ce[2 * u + s, at, :] = ce[2 * u + s, at, :] + value[u * 32 : (u + 1) * 32]
 
+    finish_sums(0, 0)
+    start_sums(0, 1)
+
     @pl.loop(0, (rows + 2) // 2)
     def _(k):
         a = 2 + 2 * k
@@ -412,6 +398,23 @@
     if reduce:
         stage_all(1, lambda d: [conv_sum[d * nc : (d + 1) * nc, :]])
     start_sums(1, 0)
+
+    co_rows = co[1 : half + 1].reshape(half * 32, wide)
+    for e in range(4):
+        p, q = e // 2, e % 2
+        res = dot(co_rows, wu[p, q]).reshape(half, 32, ch)
+        for m in range(half):
+            up[2 * m + p, pl.ds(1 + q, 32, stride=2), :] = res[m]
+
+    @pl.loop(0, rows // 4)
+    def _(k):
+        f = fine[pl.ds(3 + k * 4, 4), 3 : 3 + cols, :].astype(BF16).astype(F32)
+        out_ref[pl.ds(k * 4, 4)] = (f + up[pl.ds(k * 4, 4), 3 : 3 + cols, :]).astype(BF16)
+
+    out_copy = pltpu.make_async_copy(out_ref, out_hbm, local_sem.at[5])
+    out_copy.start()
+    finish_sums(1, 0)
+    start_sums(1, 1)
     finish_sums(0, 1)
     start_sums(0, 2)
 
@@ -433,21 +436,41 @@
         return done
 
     first_half = half_inputs(0)
-    finish_sums(1, 0)
-    start_sums(1, 1)
-    second_half = half_inputs(1)
     finish_sums(1, 1)
     start_sums(1, 2)
+    second_half = half_inputs(1)
     total = finish_sums(0, 2)
     if reduce:
         up_out[...] = total[0:nu]
-        down_out[:, 0:128] = total[nu : nu + nd]
-        down_out[:, 128:256] = total[nu + nd : nu + 2 * nd]
+        down_out[pl.ds(0, nd, stride=2), :] = total[nu : nu + nd]
+        down_out[pl.ds(1, nd, stride=2), :] = total[nu + nd : nu + 2 * nd]
     total = finish_sums(1, 2)
     if reduce:
         conv_out[...] = total[0:nc]
     for item in (out_copy, first_half, second_half):
         item.wait()
+
+
+def results_kernel(*refs):
+    n = (len(refs) - 1) // 2
+    copies = [pltpu.make_async_copy(refs[k], refs[n + k], refs[-1].at[k]) for k in range(n)]
+    for item in copies:
+        item.start()
+    for item in copies:
+        item.wait()
+
+
+def results(arrays):
+    anywhere = pl.BlockSpec(memory_space=pl.ANY)
+    return pl.pallas_call(
+        results_kernel,
+        out_shape=[jax.ShapeDtypeStruct(a.shape, a.dtype) for a in arrays],
+        in_specs=[anywhere] * len(arrays),
+        out_specs=[anywhere] * len(arrays),
+        scratch_shapes=[pltpu.SemaphoreType.DMA((len(arrays),))],
+        compiler_params=pltpu.CompilerParams(vmem_limit_bytes=60 * 2**20),
+        name="results",
+    )(*arrays)
 
 
 def body(n_row, n_col, x, ct, wc, wd, wu):
@@ -488,12 +511,12 @@
                 (blocks,), (blocks // 2,), (n_row, nz), (n_row - 1, nz), (nz,), (nz - 1,)
             ):
                 more.append(pltpu.VMEM(lead + (height, 128), BF16))
-        outs = [(n // blocks, w) for n, w in sums]
+        outs = [(n * w // blocks // 128, 128) for n, w in sums]
     else:
         outs = sums
     scratch += [pltpu.SemaphoreType.DMA((n_sems,))] * 2 + [pltpu.SemaphoreType.DMA((8,))] + more
     anywhere = pl.BlockSpec(memory_space=pl.ANY)
-    output, grad_inputs, *sums = pl.pallas_call(
+    found = pl.pallas_call(
         functools.partial(level_kernel, n_row, n_col, reduce),
         out_shape=[jax.ShapeDtypeStruct(x.shape, BF16)] * 2
         + [jax.ShapeDtypeStruct(s, F32) for s in outs],
@@ -505,6 +528,7 @@
         ),
         name="level",
     )(x, ct, wc, wd, wu)
+    output, grad_inputs, *sums = results(found)
     sums = [a.reshape(-1) for a in sums]
     if not reduce:
         scale = 1.0 / math.sqrt(rows * n_row * cols * n_col)

time: 41.9 us -> 64.7 us (1.54)
  Pallas kernels: 35.6 us -> 63.9 us
  local copies, waits for them, and re-layouts: 5.38 us -> 0 us
    pallas_call x0 -> x1, Pallas kernels: none -> 31.1 us  [results(): pl.pallas_call(results_kernel, out_shape=[jax.ShapeDtypeStruct(a.shape, a...]
    unnamed x10 -> x0, local copies, waits for them, and re-layouts: 3.98 us -> none
    pallas_call x1, Pallas kernels: 35.6 us -> 32.8 us  [body(): pl.pallas_call(functools.partial(level_kernel, n_row, n_col, reduce), out...]
    reshape x1 -> x0, local copies, waits for them, and re-layouts: 1.4 us -> none  [body(): sums = [a.reshape(-1) for a in sums]]
where the time goes in v3:
time: 64.7 us; the launch traced here: 64.6 us
  Pallas kernels  63.9 us (99%)
    pallas_call x1, Pallas kernels, body(): pl.pallas_call(functools.partial(level_kernel, n_row, n_col, reduce), out...  32.8 us
    pallas_call x1, Pallas kernels, results(): pl.pallas_call(results_kernel, out_shape=[jax.ShapeDtypeStruct(a.shape, a...  31.1 us

profile of v3, /device:TPU:0, one launch (start us, length us, event | category | flops | bytes accessed | tf_op | source)
XLA Modules:
  0.0 64.6 jit_solution(13260158976096056023)
XLA Ops:
  0.6 32.8 %level.1 = (bf16[32,56,128]{2,1,0:T(8,128)(2,1)}, bf16[32,56,128]{2,1,0:T(8,128)(2,1)}, f32[36,128]{1,0:T(8,128)}, f32[72,128]{1,0:T(8,128)}, f32[32,128]{1,0:T(8,128)}) custom-call(bf16[32,56,128]{2,1,0:T(8,128)(2,1)} %refs_0_.1, bf16[32,56,128]{2,1,0:T(8,128)(2,1)} %refs_1_.1, bf16[3,3,128,128]{3,2,1,0:T(8,128)(2,1)} %refs_2_.1, ...), custom_call_target="tpu_custom_call" | custom-call | tf_op jit(solution)/shard_map/level/pallas_call | solution.py:519
  33.5 31.1 %results.1 = (bf16[32,56,128]{2,1,0:T(8,128)(2,1)}, bf16[32,56,128]{2,1,0:T(8,128)(2,1)}, f32[36,128]{1,0:T(8,128)}, f32[72,128]{1,0:T(8,128)}, f32[32,128]{1,0:T(8,128)}) custom-call(bf16[32,56,128]{2,1,0:T(8,128)(2,1)} %get-tuple-element.15.refs_0_, bf16[32,56,128]{2,1,0:T(8,128)(2,1)} %get-tuple-element.16.refs_1_, f32[36,128]{1,0:T(8,128)} %get-tuple-element.17.refs_2_, ...), custom_call_target="tpu_custom_call" | custom-call | tf_op jit(solution)/shard_map/results/pallas_call | solution.py:465

commit v4 on v3

--- a/solution.py
+++ b/solution.py
@@ -56,8 +56,6 @@
             [(x_hbm, x_ref), (ct_hbm, ct_ref), (wc_hbm, wc), (wd_hbm, wd), (wu_hbm, wu)]
         )
     ]
-    for item in loads:
-        item.start()
 
     def near(dr, dc):
         ok = None
@@ -81,6 +79,9 @@
 
     for peer in peers:
         pl.semaphore_signal(barrier, inc=1, device_id=peer, device_id_type=MESH)
+
+    for item in loads:
+        item.start()
 
     loads[0].wait()
     loads[1].wait()
@@ -132,11 +133,21 @@
     slope[:, 64:72, :] = jnp.zeros((a_rows, 8, ch), F32)
     gp[:, 64:72, :] = jnp.zeros((a_rows, 8, ch), F32)
 
+    def shift_inputs(at, first, n):
+        for q in range(3):
+            x3[at, first : first + n, q * ch : (q + 1) * ch] = xf[
+                at, first + q : first + q + n, :
+            ].astype(BF16)
+
+    xf[:, 0:8, :] = jnp.zeros((rows + 8, 8, ch), F32)
+    xf[:, 56:64, :] = jnp.zeros((rows + 8, 8, ch), F32)
+
     @pl.loop(0, rows // 4)
     def _(k):
         at = pl.ds(k * 4, 4)
         xf[pl.ds(4 + k * 4, 4), 4 : 4 + cols, :] = x_ref[at].astype(F32)
         ce[pl.ds(2 + k * 4, 4), 3 : 3 + cols, :] = ct_ref[at].astype(F32)
+        shift_inputs(pl.ds(4 + k * 4, 4), 16, 32)
 
     for item in loads[2:]:
         item.wait()
@@ -240,13 +251,16 @@
     blocks = n_row * n_col
     nc, nd, nu = 9 * ch // blocks, 9 * ch // blocks, 4 * wide // blocks
 
-    @pl.loop(0, (rows + 8) // 4)
-    def _(k):
-        at = pl.ds(k * 4, 4)
-        for q in range(3):
-            x3[at, :, q * ch : (q + 1) * ch] = xf[at, q : q + 64, :].astype(BF16)
-
-    wc_rows = wc[...].reshape(3, 3 * ch, ch)
+    for at in (pl.ds(0, 4), pl.ds(rows + 4, 4)):
+        shift_inputs(at, 0, 64)
+
+    @pl.loop(0, rows // 8)
+    def _(k):
+        at = pl.ds(4 + k * 8, 8)
+        shift_inputs(at, 0, 16)
+        shift_inputs(at, 48, 16)
+
+    wc_rows = wc[...].reshape(9 * ch, ch)
     j_at = lax.broadcasted_iota(jnp.int32, (1, 64, 1), 1) - 3
     col_ok = jnp.logical_and(
         jnp.logical_or(j_at >= 0, has_left), jnp.logical_or(j_at < cols, has_right)
@@ -262,10 +276,10 @@
 
     @pl.loop(0, 2)
     def _(k):
-        pre = None
-        for p in range(3):
-            term = dot(x3[pl.ds(k * step + p, step)].reshape(step * 64, 3 * ch), wc_rows[p])
-            pre = term if pre is None else pre + term
+        windows = [
+            x3[pl.ds(k * step + p, step)].reshape(step * 64, 3 * ch) for p in range(3)
+        ]
+        pre = dot(jnp.concatenate(windows, axis=1), wc_rows)
         sig = jax.nn.sigmoid(pre)
         at = pl.ds(k * step, step)
         ok = in_grid(k * step, step)
@@ -290,12 +304,10 @@
                     2 * k + p, pl.ds(1 + q, 32, stride=2), :
                 ].astype(BF16)
 
-    wd_rows = wd[...].reshape(3, 3 * ch, wide)
-    cpre = None
-    for p in range(3):
-        window = d3[p // 2 : p // 2 + u_rows, p % 2].reshape(u_rows * 32, 3 * ch)
-        term = dot(window, wd_rows[p])
-        cpre = term if cpre is None else cpre + term
+    windows = [
+        d3[p // 2 : p // 2 + u_rows, p % 2].reshape(u_rows * 32, 3 * ch) for p in range(3)
+    ]
+    cpre = dot(jnp.concatenate(windows, axis=1), wd[...].reshape(9 * ch, wide))
     cp[...] = cpre.reshape(u_rows, 32, wide)
     v_at = lax.broadcasted_iota(jnp.int32, (1, 32, 1), 1) - 1
     v_own = jnp.logical_and(v_at >= 0, v_at < cols // 2)
@@ -418,16 +430,17 @@
     finish_sums(0, 1)
     start_sums(0, 2)
 
-    turned = [jnp.concatenate([wc[p, q] for q in range(3)], axis=1) for p in range(3)]
+    turned = jnp.concatenate([wc[p, q] for p in range(3) for q in range(3)], axis=1)
     part_rows = rows // 2
 
     def half_inputs(k):
-        total = None
-        for p in range(3):
-            first = k * part_rows + 4 - p
-            window = g3[first : first + part_rows].reshape(part_rows * 64, 3 * ch)
-            term = dot_nt(window, turned[p])
-            total = term if total is None else total + term
+        windows = [
+            g3[k * part_rows + 4 - p : (k + 1) * part_rows + 4 - p].reshape(
+                part_rows * 64, 3 * ch
+            )
+            for p in range(3)
+        ]
+        total = dot_nt(jnp.concatenate(windows, axis=1), turned)
         total = total.reshape(part_rows, 64, ch)[:, :cols, :]
         at = pl.ds(k * part_rows, part_rows)
         gx_ref[at] = total.astype(BF16)
@@ -451,23 +464,40 @@
         item.wait()
 
 
-def results_kernel(*refs):
-    n = (len(refs) - 1) // 2
-    copies = [pltpu.make_async_copy(refs[k], refs[n + k], refs[-1].at[k]) for k in range(n)]
-    for item in copies:
+def results_kernel(n, *refs):
+    given, out, held, (in_sem, out_sem) = refs[:n], refs[n : 2 * n], refs[2 * n : 3 * n], refs[3 * n :]
+    pieces = []
+    for k in range(n):
+        size = given[k].shape[0]
+        step = size // 2 if len(given[k].shape) == 3 else size
+        pieces += [(k, pl.ds(at, step)) for at in range(0, size, step)]
+    loads = [
+        pltpu.make_async_copy(given[k].at[at], held[k].at[at], in_sem.at[m])
+        for m, (k, at) in enumerate(pieces)
+    ]
+    stores = [
+        pltpu.make_async_copy(held[k].at[at], out[k].at[at], out_sem.at[m])
+        for m, (k, at) in enumerate(pieces)
+    ]
+    for item in loads:
         item.start()
-    for item in copies:
+    for load, store in zip(loads, stores):
+        load.wait()
+        store.start()
+    for item in stores:
         item.wait()
 
 
 def results(arrays):
     anywhere = pl.BlockSpec(memory_space=pl.ANY)
+    n = len(arrays)
     return pl.pallas_call(
-        results_kernel,
+        functools.partial(results_kernel, n),
         out_shape=[jax.ShapeDtypeStruct(a.shape, a.dtype) for a in arrays],
-        in_specs=[anywhere] * len(arrays),
-        out_specs=[anywhere] * len(arrays),
-        scratch_shapes=[pltpu.SemaphoreType.DMA((len(arrays),))],
+        in_specs=[anywhere] * n,
+        out_specs=[anywhere] * n,
+        scratch_shapes=[pltpu.VMEM(a.shape, a.dtype) for a in arrays]
+        + [pltpu.SemaphoreType.DMA((2 * n,))] * 2,
         compiler_params=pltpu.CompilerParams(vmem_limit_bytes=60 * 2**20),
         name="results",
     )(*arrays)

time: 64.7 us -> 35.3 us (0.55)
  Pallas kernels: 63.9 us -> 34.5 us
    pallas_call x1, Pallas kernels: 31.1 us -> 2.16 us  [results(): pl.pallas_call(functools.partial(results_kernel, n), out_shape=[jax.Shape...]
where the time goes in v4:
time: 35.3 us; the launch traced here: 35.1 us
  Pallas kernels  34.5 us (98%)
  between operations  0.64 us (2%)
    pallas_call x1, Pallas kernels, body(): pl.pallas_call(functools.partial(level_kernel, n_row, n_col, reduce), out...  32.3 us
    pallas_call x1, Pallas kernels, results(): pl.pallas_call(functools.partial(results_kernel, n), out_shape=[jax.Shape...  2.16 us

profile of v4, /device:TPU:0, one launch (start us, length us, event | category | flops | bytes accessed | tf_op | source)
XLA Modules:
  0.0 35.1 jit_solution(15859985669103853764)
XLA Ops:
  0.6 32.3 %level.1 = (bf16[32,56,128]{2,1,0:T(8,128)(2,1)}, bf16[32,56,128]{2,1,0:T(8,128)(2,1)}, f32[36,128]{1,0:T(8,128)}, f32[72,128]{1,0:T(8,128)}, f32[32,128]{1,0:T(8,128)}) custom-call(bf16[32,56,128]{2,1,0:T(8,128)(2,1)} %refs_0_.1, bf16[32,56,128]{2,1,0:T(8,128)(2,1)} %refs_1_.1, bf16[3,3,128,128]{3,2,1,0:T(8,128)(2,1)} %refs_2_.1, ...), custom_call_target="tpu_custom_call" | custom-call | tf_op jit(solution)/shard_map/level/pallas_call | solution.py:549
  32.9 2.2 %results.1 = (bf16[32,56,128]{2,1,0:T(8,128)(2,1)}, bf16[32,56,128]{2,1,0:T(8,128)(2,1)}, f32[36,128]{1,0:T(8,128)}, f32[72,128]{1,0:T(8,128)}, f32[32,128]{1,0:T(8,128)}) custom-call(bf16[32,56,128]{2,1,0:T(8,128)(2,1)} %get-tuple-element.15.refs_0_, bf16[32,56,128]{2,1,0:T(8,128)(2,1)} %get-tuple-element.16.refs_1_, f32[36,128]{1,0:T(8,128)} %get-tuple-element.17.refs_2_, ...), custom_call_target="tpu_custom_call" | custom-call | tf_op jit(solution)/shard_map/results/pallas_call | solution.py:494

commit v5 on v4

--- a/solution.py
+++ b/solution.py
@@ -383,12 +383,6 @@
         value = ce[pl.ds(a - 1, 2), 0:64, :] * slope[pl.ds(a, 2), 0:64, :]
         gp[pl.ds(a, 2), 0:64, :] = jnp.where(in_grid(a, 2), value, 0.0)
 
-    @pl.loop(0, (rows + 2) // 2)
-    def _(k):
-        at = pl.ds(2 + 2 * k, 2)
-        for q in range(3):
-            g3[at, :, q * ch : (q + 1) * ch] = gp[at, 4 - q : 68 - q, :].astype(BF16)
-
     j_own = jnp.logical_and(j_at >= 0, j_at < cols)
     own = jnp.where(j_own, gp[3 : rows + 3, 0:64, :], 0.0).astype(BF16)
 
@@ -410,6 +404,12 @@
     if reduce:
         stage_all(1, lambda d: [conv_sum[d * nc : (d + 1) * nc, :]])
     start_sums(1, 0)
+
+    @pl.loop(0, (rows + 2) // 2)
+    def _(k):
+        at = pl.ds(2 + 2 * k, 2)
+        for q in range(3):
+            g3[at, :, q * ch : (q + 1) * ch] = gp[at, 4 - q : 68 - q, :].astype(BF16)
 
     co_rows = co[1 : half + 1].reshape(half * 32, wide)
     for e in range(4):

time: 35.3 us -> 35.3 us (level)
  no operation moved by 1% of the time
where the time goes in v5:
time: 35.3 us; the launch traced here: 35.1 us
  Pallas kernels  34.5 us (98%)
  between operations  0.64 us (2%)
    pallas_call x1, Pallas kernels, body(): pl.pallas_call(functools.partial(level_kernel, n_row, n_col, reduce), out...  32.3 us
    pallas_call x1, Pallas kernels, results(): pl.pallas_call(functools.partial(results_kernel, n), out_shape=[jax.Shape...  2.16 us

profile of v5, /device:TPU:0, one launch (start us, length us, event | category | flops | bytes accessed | tf_op | source)
XLA Modules:
  0.0 35.1 jit_solution(6336978895540998621)
XLA Ops:
  0.6 32.3 %level.1 = (bf16[32,56,128]{2,1,0:T(8,128)(2,1)}, bf16[32,56,128]{2,1,0:T(8,128)(2,1)}, f32[36,128]{1,0:T(8,128)}, f32[72,128]{1,0:T(8,128)}, f32[32,128]{1,0:T(8,128)}) custom-call(bf16[32,56,128]{2,1,0:T(8,128)(2,1)} %refs_0_.1, bf16[32,56,128]{2,1,0:T(8,128)(2,1)} %refs_1_.1, bf16[3,3,128,128]{3,2,1,0:T(8,128)(2,1)} %refs_2_.1, ...), custom_call_target="tpu_custom_call" | custom-call | tf_op jit(solution)/shard_map/level/pallas_call | solution.py:549
  32.9 2.2 %results.1 = (bf16[32,56,128]{2,1,0:T(8,128)(2,1)}, bf16[32,56,128]{2,1,0:T(8,128)(2,1)}, f32[36,128]{1,0:T(8,128)}, f32[72,128]{1,0:T(8,128)}, f32[32,128]{1,0:T(8,128)}) custom-call(bf16[32,56,128]{2,1,0:T(8,128)(2,1)} %get-tuple-element.15.refs_0_, bf16[32,56,128]{2,1,0:T(8,128)(2,1)} %get-tuple-element.16.refs_1_, f32[36,128]{1,0:T(8,128)} %get-tuple-element.17.refs_2_, ...), custom_call_target="tpu_custom_call" | custom-call | tf_op jit(solution)/shard_map/results/pallas_call | solution.py:494

commit v6 on v5

--- a/solution.py
+++ b/solution.py
@@ -411,6 +411,11 @@
         for q in range(3):
             g3[at, :, q * ch : (q + 1) * ch] = gp[at, 4 - q : 68 - q, :].astype(BF16)
 
+    finish_sums(1, 0)
+    start_sums(1, 1)
+    finish_sums(0, 1)
+    start_sums(0, 2)
+
     co_rows = co[1 : half + 1].reshape(half * 32, wide)
     for e in range(4):
         p, q = e // 2, e % 2
@@ -425,11 +430,6 @@
 
     out_copy = pltpu.make_async_copy(out_ref, out_hbm, local_sem.at[5])
     out_copy.start()
-    finish_sums(1, 0)
-    start_sums(1, 1)
-    finish_sums(0, 1)
-    start_sums(0, 2)
-
     turned = jnp.concatenate([wc[p, q] for p in range(3) for q in range(3)], axis=1)
     part_rows = rows // 2
 

time: 35.3 us -> 35.4 us (level)
  no operation moved by 1% of the time
where the time goes in v6:
time: 35.4 us; the launch traced here: 35.2 us
  Pallas kernels  34.6 us (98%)
  between operations  0.64 us (2%)
    pallas_call x1, Pallas kernels, body(): pl.pallas_call(functools.partial(level_kernel, n_row, n_col, reduce), out...  32.4 us
    pallas_call x1, Pallas kernels, results(): pl.pallas_call(functools.partial(results_kernel, n), out_shape=[jax.Shape...  2.16 us

profile of v6, /device:TPU:0, one launch (start us, length us, event | category | flops | bytes accessed | tf_op | source)
XLA Modules:
  0.0 35.2 jit_solution(530271297189782246)
XLA Ops:
  0.6 32.4 %level.1 = (bf16[32,56,128]{2,1,0:T(8,128)(2,1)}, bf16[32,56,128]{2,1,0:T(8,128)(2,1)}, f32[36,128]{1,0:T(8,128)}, f32[72,128]{1,0:T(8,128)}, f32[32,128]{1,0:T(8,128)}) custom-call(bf16[32,56,128]{2,1,0:T(8,128)(2,1)} %refs_0_.1, bf16[32,56,128]{2,1,0:T(8,128)(2,1)} %refs_1_.1, bf16[3,3,128,128]{3,2,1,0:T(8,128)(2,1)} %refs_2_.1, ...), custom_call_target="tpu_custom_call" | custom-call | tf_op jit(solution)/shard_map/level/pallas_call | solution.py:549
  33.1 2.2 %results.1 = (bf16[32,56,128]{2,1,0:T(8,128)(2,1)}, bf16[32,56,128]{2,1,0:T(8,128)(2,1)}, f32[36,128]{1,0:T(8,128)}, f32[72,128]{1,0:T(8,128)}, f32[32,128]{1,0:T(8,128)}) custom-call(bf16[32,56,128]{2,1,0:T(8,128)(2,1)} %get-tuple-element.15.refs_0_, bf16[32,56,128]{2,1,0:T(8,128)(2,1)} %get-tuple-element.16.refs_1_, f32[36,128]{1,0:T(8,128)} %get-tuple-element.17.refs_2_, ...), custom_call_target="tpu_custom_call" | custom-call | tf_op jit(solution)/shard_map/results/pallas_call | solution.py:494
